TPU v7x, 256 devices: a whole 4x4x8 slice. The times are simulated.
256 devices in a mesh: row: 32 (over z, x), col: 8 (over y, core).
Axes of the slice: x: 4, y: 4, z: 8, core: 2. Of those that a mesh axis runs over, the one named last changes fastest.
Arguments:
- sources: float32 [128, 65536], P('col', 'row'), may hold values from -6 to 6
- tiles: bfloat16 [32, 8, 48, 256, 256], P('row', 'col')
- tile_row: int32 [32, 8, 48], P('row', 'col'), may hold values from 0 to 7
- tile_col: int32 [32, 8, 48], P('row', 'col'), may hold values from 0 to 31
- tile_count: int32 [32, 8], P('row', 'col'), may hold values from 1 to 48, as said below
Outputs:
- potential: float32 [128, 65536], P('col', 'row')
Inputs may be any that keep to these rules, and one draw needn't show every extreme that they name: `tile_count`: slots at or past a device's count hold no part of the operator; some device holds exactly 48 live slots; tile pairs may repeat and then add.
All inputs are finite; a program needn't handle non-finite values.
Results may differ from a plain program's by a relative error of at most 0.0029.
Values may be sent and summed in bfloat16 or wider, within the bound.
A program may use at most 128 MiB of HBM per device.

v0:
```python
import math

import jax
import jax.numpy as jnp
import numpy as np
from jax import lax
from jax.sharding import PartitionSpec as P

ROOT_HALF = 1.0 / math.sqrt(2.0)
tile_group = 8


def swapped(value, axis, apart):
    mask = 2**apart
    pairs = [(source, source ^ mask) for source in range(lax.axis_size(axis))]
    return lax.ppermute(value, axis, pairs)


def haar_table(extent):
    matrix = np.eye(extent)
    stride = 1
    while stride < extent:
        for position in range(0, extent, 2 * stride):
            first_row = matrix[position].copy()
            second_row = matrix[position + stride].copy()
            matrix[position] = (first_row + second_row) * ROOT_HALF
            matrix[position + stride] = (first_row - second_row) * ROOT_HALF
        stride = stride * 2
    return matrix


def pair_step(values, stride):
    height, extent = values.shape
    shaped = values.reshape(height, extent // (2 * stride), 2, stride)
    first_part = shaped[:, :, 0, 0]
    second_part = shaped[:, :, 1, 0]
    shaped = shaped.at[:, :, 0, 0].set((first_part + second_part) * ROOT_HALF)
    shaped = shaped.at[:, :, 1, 0].set((first_part - second_part) * ROOT_HALF)
    return shaped.reshape(height, extent)


def haar_forward(values):
    stride = 1
    while stride < values.shape[1]:
        values = pair_step(values, stride)
        stride = stride * 2
    return values


def haar_inverse(values):
    stride = values.shape[1] // 2
    while stride >= 1:
        values = pair_step(values, stride)
        stride = stride // 2
    return values


def butterfly(coarse_value, partner, row_index, level_bit):
    active = row_index % 2**level_bit == 0
    upper_half = row_index // 2**level_bit % 2 == 1
    combined = jnp.where(upper_half, partner - coarse_value, partner + coarse_value) * ROOT_HALF
    return jnp.where(active, combined, coarse_value)


def forward_cross(coarse_value, row_index):
    bit_count = lax.axis_size("row").bit_length() - 1
    for level_bit in range(bit_count):
        partner = swapped(coarse_value, "row", level_bit)
        coarse_value = butterfly(coarse_value, partner, row_index, level_bit)
    return coarse_value


def inverse_cross(coarse_value, row_index):
    bit_count = lax.axis_size("row").bit_length() - 1
    for level_bit in reversed(range(bit_count)):
        partner = swapped(coarse_value, "row", level_bit)
        coarse_value = butterfly(coarse_value, partner, row_index, level_bit)
    return coarse_value


def local(sources, tiles, tile_row, tile_col, tile_count):
    extent = tiles.shape[-1]
    height = sources.shape[0]
    blocks = sources.shape[1] // extent
    haar_matrix = jnp.asarray(haar_table(extent), jnp.float32)
    row_index = lax.axis_index("row")
    col_index = lax.axis_index("col")
    shaped = sources.reshape(height, blocks, extent)
    local_coef = jnp.einsum("rbk,nk->rbn", shaped, haar_matrix, precision=lax.Precision.HIGHEST)
    scaling = haar_forward(local_coef[:, :, 0])
    first_value = scaling[:, 0:1]
    first_value = forward_cross(first_value, row_index)
    scaling = scaling.at[:, 0:1].set(first_value)
    wavelet = local_coef.at[:, :, 0].set(scaling).astype(jnp.bfloat16)
    all_sides = lax.all_gather(wavelet, "col", axis=0, tiled=True)
    owners = lax.axis_size("row") // lax.axis_size("col")
    group_blocks = blocks * owners
    every_block = lax.all_gather(all_sides, "row", axis=1, tiled=True)
    needed = lax.dynamic_slice_in_dim(every_block, col_index * group_blocks, group_blocks, 1)
    tile_stack = tiles.reshape(tiles.shape[2], extent, extent)
    rows_flat = tile_row.reshape(-1)
    cols_flat = tile_col.reshape(-1)
    live_count = tile_count.reshape(())
    groups = (live_count + tile_group - 1) // tile_group
    block_range = jnp.arange(blocks, dtype=jnp.int32)
    slot_range = jnp.arange(tile_group, dtype=jnp.int32)

    def accumulate(group_index, running):
        first_slot = group_index * tile_group
        group_tiles = lax.dynamic_slice_in_dim(tile_stack, first_slot, tile_group, 0)
        group_rows = lax.dynamic_slice_in_dim(rows_flat, first_slot, tile_group, 0)
        group_cols = lax.dynamic_slice_in_dim(cols_flat, first_slot, tile_group, 0)
        gathered_sides = jnp.take(needed, group_cols, axis=1)
        product = jnp.einsum(
            "rtk,tkn->rtn", gathered_sides, group_tiles, preferred_element_type=jnp.float32
        )
        usable = first_slot + slot_range < live_count
        select = ((group_rows[:, None] == block_range[None, :]) & usable[:, None]).astype(
            jnp.float32
        )
        return running + jnp.einsum("ti,rtn->rin", select, product, precision=lax.Precision.HIGHEST)

    image_coef = lax.psum_scatter(
        lax.fori_loop(
            0,
            groups,
            accumulate,
            jnp.zeros((height * lax.axis_size("col"), blocks, extent), jnp.float32),
        ),
        "col",
        scatter_dimension=0,
        tiled=True,
    )
    back_scaling = image_coef[:, :, 0]
    top_value = back_scaling[:, 0:1]
    top_value = inverse_cross(top_value, row_index)
    back_scaling = back_scaling.at[:, 0:1].set(top_value)
    back_scaling = haar_inverse(back_scaling)
    image_coef = image_coef.at[:, :, 0].set(back_scaling)
    result = jnp.einsum("rbn,nk->rbk", image_coef, haar_matrix, precision=lax.Precision.HIGHEST)
    return result.reshape(height, blocks * extent)


def solution(mesh):
    return jax.shard_map(
        local,
        mesh=mesh,
        in_specs=(
            P("col", "row"),
            P("row", "col", None, None, None),
            P("row", "col", None),
            P("row", "col", None),
            P("row", "col"),
        ),
        out_specs=P("col", "row"),
        check_vma=False,
    )
```

profile of v0, /device:TPU:2, one launch (start us, length us, event | category | flops | bytes accessed | tf_op | source)
XLA Modules:
  0.0 298.3 jit_solution(15067728782173562360)
XLA Ops:
  8.3 2.3 collective-permute-start
  12.2 1.9 collective-permute-start.1
  14.0 3.2 %collective-permute-done.1 = f32[16,1]{0,1:T(1,128)S(1)} collective-permute-done((f32[16,1]{0,1:T(1,128)S(1)}, f32[16,1]{0,1:T(1,128)S(1)}, u32[]{:S(2)}, u32[]{:S(2)}) %collective-permute-start.1) | collective-permute-done | bytes 96 | tf_op jit(solution)/shard_map/ppermute | solution.py:16
  18.9 1.9 collective-permute-done.2
  20.8 3.0 %collective-permute-start.3 = (f32[16,1]{0,1:T(1,128)S(1)}, f32[16,1]{0,1:T(1,128)S(1)}, u32[]{:S(2)}, u32[]{:S(2)}) collective-permute-start(f32[16,1]{0,1:T(1,128)S(1)} %broadcast_select_fusion.9), channel_id=1, source_target_pairs={{0,64},{8,72},{16,80},{24,88},{32,96},{40,104},{48,112},{56,120},{... | collective-permute-start | bytes 200 | tf_op jit(solution)/shard_map/ppermute | solution.py:16
  25.3 6.8 %collective-permute-start.4 = (f32[16,1]{0,1:T(1,128)S(1)}, f32[16,1]{0,1:T(1,128)S(1)}, u32[]{:S(2)}, u32[]{:S(2)}) collective-permute-start(f32[16,1]{0,1:T(1,128)S(1)} %broadcast_select_fusion.13), channel_id=1, source_target_pairs={{0,128},{8,136},{16,144},{24,152},{32,160},{40,168},{48,176},{56,1... | collective-permute-start | bytes 200 | tf_op jit(solution)/shard_map/ppermute | solution.py:16
  34.5 14.7 %all_gather.6 = bf16[128,8,256]{2,0,1:T(8,128)(2,1)} all-gather(bf16[16,8,256]{2,0,1:T(8,128)(2,1)S(1)} %convert_element_type.5), channel_id=1, replica_groups=mesh['row'=32,'col'=8] {'col'}, dimensions={0}, use_global_device_ids=true | all-gather | bytes 589824 | tf_op jit(solution)/shard_map/all_gather | solution.py:95
  50.0 8.7 %copy.26 = bf16[1,1,48,256,256]{3,4,2,1,0:T(8,128)(2,1)} copy(bf16[1,1,48,256,256]{4,3,2,1,0:T(8,128)(2,1)} %param.41) | data formatting | bytes 12582912 | tf_op args[1]
  58.7 131.1 %all-gather.2.cloned.1.call-done = bf16[128,256,256]{2,0,1:T(8,128)(2,1)} async-done(((bf16[128,8,256]{2,0,1:T(8,128)(2,1)}), bf16[128,256,256]{2,0,1:T(8,128)(2,1)}) %all-gather.2.cloned.1.call-update) | async-done | bytes 16777232 | tf_op jit(solution)/shard_map/all_gather | solution.py:98
  189.7 3.2 %constant_dynamic-slice_fusion = bf16[128,32,256]{2,0,1:T(8,128)(2,1)} fusion(bf16[128,256,256]{2,0,1:T(8,128)(2,1)} %all-gather.2.cloned.1.call-done, s32[]{:T(128)S(6)} %select_n.228), kind=kLoop, calls=%fused_computation.71 | loop fusion | bytes 4194308 | tf_op jit(solution)/shard_map/dynamic_slice | solution.py:99
  193.0 18.3 %while.29 = (s32[]{:T(128)}, f32[128,8,256]{2,1,0:T(8,128)S(1)}, s32[]{:T(128)}, bf16[48,256,256]{1,2,0:T(8,128)(2,1)}, s32[48]{0:T(128)S(1)}, /*index=5*/bf16[1...) while((s32[]{:T(128)}, f32[128,8,256]{2,1,0:T(8,128)S(1)}, ...), condition=%wide.region_2.0_spmd.clone.clone, body=%wide.region_1.0_spmd.clone.clone.sunk | while | flops 159909056 | bytes 8917431 | solution.py:124
  193.8 2.2 gather_fusion
  199.9 2.2 gather_fusion
  202.1 1.7 convolution_bitcast_fusion.4
  206.0 2.2 gather_fusion
  212.3 49.7 %reduce-scatter.2.cloned.1.call-done = f32[16,8,256]{2,1,0:T(8,128)} async-done(((f32[128,8,256]{2,1,0:T(8,128)}), f32[16,8,256]{2,1,0:T(8,128)}) %reduce-scatter.2.cloned.1.call-update) | async-done | bytes 131088 | tf_op jit(solution)/shard_map/reduce_scatter | solution.py:123
  262.9 5.7 %collective-permute-start.5 = (f32[16,1]{0,1:T(1,128)S(1)}, f32[16,1]{0,1:T(1,128)S(1)}, u32[]{:S(2)}, u32[]{:S(2)}) collective-permute-start(f32[16,1]{0,1:T(1,128)S(1)} %slice.460), channel_id=1, source_target_pairs={{0,128},{8,136},{16,144},{24,152},{32,160},{40,168},{48,176},{56,1... | collective-permute-start | bytes 200 | tf_op jit(solution)/shard_map/ppermute | solution.py:16
  268.7 1.8 collective-permute-done.5
  270.4 2.5 collective-permute-start.6
  273.0 1.9 collective-permute-done.6
  276.4 2.0 collective-permute-done.7
  278.4 2.0 collective-permute-start.8
  280.5 3.0 %collective-permute-done.8 = f32[16,1]{0,1:T(1,128)S(1)} collective-permute-done((f32[16,1]{0,1:T(1,128)S(1)}, f32[16,1]{0,1:T(1,128)S(1)}, u32[]{:S(2)}, u32[]{:S(2)}) %collective-permute-start.8) | collective-permute-done | bytes 96 | tf_op jit(solution)/shard_map/ppermute | solution.py:16
  285.1 1.9 collective-permute-done.9
  (82 shorter events, 28.3 us)
Async XLA Ops:
  6.5 183.2 %all-gather.2.cloned.1.call-start = ((), (), s32[]{:S(2)}) async-start(), calls=%async_computation.1 | async-start | bytes 17301504 | tf_op jit(solution)/shard_map/all_gather | solution.py:98
  8.3 3.9 %collective-permute-start = (f32[16,1]{0,1:T(1,128)S(1)}, f32[16,1]{0,1:T(1,128)S(1)}, u32[]{:S(2)}, u32[]{:S(2)}) collective-permute-start(f32[16,1]{0,1:T(1,128)S(1)} %slice.458), channel_id=1, source_target_pairs={{0,8},{8,0},{16,24},{24,16},{32,40},{40,32},{48,56},{56,48},{64,72... | collective-permute-start | bytes 200 | tf_op jit(solution)/shard_map/ppermute | solution.py:16
  12.2 5.0 %collective-permute-start.1 = (f32[16,1]{0,1:T(1,128)S(1)}, f32[16,1]{0,1:T(1,128)S(1)}, u32[]{:S(2)}, u32[]{:S(2)}) collective-permute-start(f32[16,1]{0,1:T(1,128)S(1)} %fusion.27), channel_id=1, source_target_pairs={{0,16},{8,24},{16,0},{24,8},{32,48},{40,56},{48,32},{56,40},{64,80... | collective-permute-start | bytes 200 | tf_op jit(solution)/shard_map/ppermute | solution.py:16
  17.2 3.5 %collective-permute-start.2 = (f32[16,1]{0,1:T(1,128)S(1)}, f32[16,1]{0,1:T(1,128)S(1)}, u32[]{:S(2)}, u32[]{:S(2)}) collective-permute-start(f32[16,1]{0,1:T(1,128)S(1)} %broadcast_select_fusion.5), channel_id=1, source_target_pairs={{0,32},{8,40},{16,48},{24,56},{32,0},{40,8},{48,16},{56,24},{64,96... | collective-permute-start | bytes 200 | tf_op jit(solution)/shard_map/ppermute | solution.py:16
  20.8 4.5 %collective-permute-start.3 = (f32[16,1]{0,1:T(1,128)S(1)}, f32[16,1]{0,1:T(1,128)S(1)}, u32[]{:S(2)}, u32[]{:S(2)}) collective-permute-start(f32[16,1]{0,1:T(1,128)S(1)} %broadcast_select_fusion.9), channel_id=1, source_target_pairs={{0,64},{8,72},{16,80},{24,88},{32,96},{40,104},{48,112},{56,120},{... | collective-permute-start | bytes 200 | tf_op jit(solution)/shard_map/ppermute | solution.py:16
  25.3 8.4 %collective-permute-start.4 = (f32[16,1]{0,1:T(1,128)S(1)}, f32[16,1]{0,1:T(1,128)S(1)}, u32[]{:S(2)}, u32[]{:S(2)}) collective-permute-start(f32[16,1]{0,1:T(1,128)S(1)} %broadcast_select_fusion.13), channel_id=1, source_target_pairs={{0,128},{8,136},{16,144},{24,152},{32,160},{40,168},{48,176},{56,1... | collective-permute-start | bytes 200 | tf_op jit(solution)/shard_map/ppermute | solution.py:16
  49.3 212.7 %reduce-scatter.2.cloned.1.call-start = ((), (), s32[]{:S(2)}) async-start(), calls=%async_computation.2 | async-start | bytes 1179648 | tf_op jit(solution)/shard_map/reduce_scatter | solution.py:123
  50.0 143.0 %copy-start.2 = (s32[1,1,48]{2,1,0:T(1,128)S(1)}, s32[1,1,48]{2,1,0:T(1,128)}, u32[]{:S(2)}) copy-start(s32[1,1,48]{2,1,0:T(1,128)} %param.43) | copy-start | bytes 580
  50.0 143.0 %copy-start.3 = (s32[1,1,48]{2,1,0:T(1,128)S(1)}, s32[1,1,48]{2,1,0:T(1,128)}, u32[]{:S(2)}) copy-start(s32[1,1,48]{2,1,0:T(1,128)} %param.42) | copy-start | bytes 580
  193.0 96.6 %copy-start.1 = (f32[256,256,1]{1,0,2:T(8,128)S(1)}, f32[256,256,1]{1,0,2:T(8,128)}, u32[]{:S(2)}) copy-start(f32[256,256,1]{1,0,2:T(8,128)} %constant.591) | copy-start | bytes 786436
  211.3 1.0 copy-start
  262.9 7.5 %collective-permute-start.5 = (f32[16,1]{0,1:T(1,128)S(1)}, f32[16,1]{0,1:T(1,128)S(1)}, u32[]{:S(2)}, u32[]{:S(2)}) collective-permute-start(f32[16,1]{0,1:T(1,128)S(1)} %slice.460), channel_id=1, source_target_pairs={{0,128},{8,136},{16,144},{24,152},{32,160},{40,168},{48,176},{56,1... | collective-permute-start | bytes 200 | tf_op jit(solution)/shard_map/ppermute | solution.py:16
  270.4 4.4 %collective-permute-start.6 = (f32[16,1]{0,1:T(1,128)S(1)}, f32[16,1]{0,1:T(1,128)S(1)}, u32[]{:S(2)}, u32[]{:S(2)}) collective-permute-start(f32[16,1]{0,1:T(1,128)S(1)} %broadcast_select_fusion.16), channel_id=1, source_target_pairs={{0,64},{8,72},{16,80},{24,88},{32,96},{40,104},{48,112},{56,120},{... | collective-permute-start | bytes 200 | tf_op jit(solution)/shard_map/ppermute | solution.py:16
  274.9 3.5 %collective-permute-start.7 = (f32[16,1]{0,1:T(1,128)S(1)}, f32[16,1]{0,1:T(1,128)S(1)}, u32[]{:S(2)}, u32[]{:S(2)}) collective-permute-start(f32[16,1]{0,1:T(1,128)S(1)} %broadcast_select_fusion.12), channel_id=1, source_target_pairs={{0,32},{8,40},{16,48},{24,56},{32,0},{40,8},{48,16},{56,24},{64,96... | collective-permute-start | bytes 200 | tf_op jit(solution)/shard_map/ppermute | solution.py:16
  278.4 5.0 %collective-permute-start.8 = (f32[16,1]{0,1:T(1,128)S(1)}, f32[16,1]{0,1:T(1,128)S(1)}, u32[]{:S(2)}, u32[]{:S(2)}) collective-permute-start(f32[16,1]{0,1:T(1,128)S(1)} %broadcast_select_fusion.8), channel_id=1, source_target_pairs={{0,16},{8,24},{16,0},{24,8},{32,48},{40,56},{48,32},{56,40},{64,80... | collective-permute-start | bytes 200 | tf_op jit(solution)/shard_map/ppermute | solution.py:16
  283.5 3.5 %collective-permute-start.9 = (f32[16,1]{0,1:T(1,128)S(1)}, f32[16,1]{0,1:T(1,128)S(1)}, u32[]{:S(2)}, u32[]{:S(2)}) collective-permute-start(f32[16,1]{0,1:T(1,128)S(1)} %broadcast_select_fusion.4), channel_id=1, source_target_pairs={{0,8},{8,0},{16,24},{24,16},{32,40},{40,32},{48,56},{56,48},{64,72... | collective-permute-start | bytes 200 | tf_op jit(solution)/shard_map/ppermute | solution.py:16
Sparse Core Ops, SparseCore 0:
  49.4 140.3 all-gather.1
  212.4 49.4 reduce-scatter.1
where the time goes:
time: 299 us; the launch traced here: 298 us
  waiting for transfers between devices  200 us (67%)
  starting transfers between devices  28.2 us (9%)
  local copies, waits for them, and re-layouts  26.2 us (9%)
  blocking collectives  14.7 us (5%)
  between operations  14.2 us (5%)
  matrix products  10.2 us (3%)
  other arithmetic  4.28 us (1%)
    all_gather x1, waiting for transfers between devices, local(): every_block = lax.all_gather(all_sides, 'row', axis=1, tiled=True)  131 us
    reduce_scatter x1, waiting for transfers between devices, local(): lax.psum_scatter(lax.fori_loop(0, groups, accumulate, jnp.zeros((height *...  49.7 us
    ppermute x10, starting transfers between devices, swapped(): return lax.ppermute(value, axis, pairs)  28.2 us
    ppermute x10, waiting for transfers between devices, swapped(): return lax.ppermute(value, axis, pairs)  19.4 us
    all_gather x1, blocking collectives, local(): all_sides = lax.all_gather(wavelet, 'col', axis=0, tiled=True)  14.7 us
    unnamed x11, local copies, waits for them, and re-layouts  10.5 us
    gather x3, local copies, waits for them, and re-layouts, accumulate(): gathered_sides = jnp.take(needed, group_cols, axis=1)  6.51 us
  transfers between devices with their start and end apart: 12, of which 12 were waited for; matrix products, arithmetic and copies ran while one was open for 4% of the time, Pallas kernels for 0%

commit v1 on v0

v1 whole, which is shorter than its diff:
```python
import math

import jax
import jax.numpy as jnp
import numpy as np
from jax import lax
from jax.experimental import pallas as pl
from jax.experimental.pallas import tpu as pltpu
from jax.sharding import PartitionSpec as P

MESH = pl.DeviceIdType.MESH
ROOT_HALF = 1.0 / math.sqrt(2.0)
NX, NY, NZ, NK = 4, 4, 8, 2
NROW, NCOL = NX * NZ, NY * NK
TILE = 256
RHS = 16
RB = 8
SLOTS = 48
HALF = RB // 2
LEVELS = 5


def sign_table(extent):
    signs = np.zeros((extent, extent), np.float32)
    factor = np.zeros((extent,), np.float64)
    signs[0] = 1.0
    factor[0] = extent**-0.5
    for n in range(1, extent):
        low = n & -n
        signs[n, n - low : n] = 1.0
        signs[n, n : n + low] = -1.0
        factor[n] = (2.0 * low) ** -0.5
    return signs, factor.astype(np.float32)


def split_dot(values, matrix):
    m = values.shape[0]
    hi = values.astype(jnp.bfloat16)
    rest = values - hi.astype(jnp.float32)
    mid = rest.astype(jnp.bfloat16)
    low = (rest - mid.astype(jnp.float32)).astype(jnp.bfloat16)
    stacked = jnp.concatenate([hi, mid, low], axis=0)
    out = jnp.dot(stacked, matrix, preferred_element_type=jnp.float32)
    return out[:m] + (out[m : 2 * m] + out[2 * m :])


def kernel(
    src_hbm, tiles_hbm, trow, tcol, tcnt, st_ref, s_ref, fac_ref,
    out_ref,
    src, tiles, wav, xa, xb, run, part, recvk, psum, ysend, yrecv, image,
    fsend, frecv, facc, tsend, trecv, prev, last,
    ld_sem, f_ss, f_rs, a_ss, a_rs, l_sem, b_ss, b_rs, r_ss, r_rs, k_ss, k_rs, y_ss, y_rs, t_ss, t_rs,
):
    r = lax.axis_index("row")
    c = lax.axis_index("col")
    x, z = lax.rem(r, NX), r // NX
    y, k = c // NK, lax.rem(c, NK)
    xs = (xa, xb)

    bar = pltpu.get_barrier_semaphore()

    def signal_row(j, carry):
        pl.semaphore_signal(bar, inc=1, device_id=(lax.rem(r + j, NROW), c), device_id_type=MESH)
        return carry

    lax.fori_loop(1, NROW, signal_row, 0)

    def signal_source(j, carry):
        @pl.when(jnp.logical_not(jnp.logical_and(z == c, j == c)))
        def _():
            pl.semaphore_signal(bar, inc=1, device_id=(c * NX + x, j), device_id_type=MESH)

        return carry

    lax.fori_loop(0, NCOL, signal_source, 0)
    pl.semaphore_signal(bar, inc=1, device_id=(r, y * NK + 1 - k), device_id_type=MESH)
    for d in range(1, NY):
        pl.semaphore_signal(bar, inc=1, device_id=(r, lax.rem(y + d, NY) * NK + k), device_id_type=MESH)

    load_src = pltpu.make_async_copy(src_hbm, src, ld_sem.at[0])
    load_src.start()
    load_tiles = pltpu.make_async_copy(tiles_hbm.at[0, 0], tiles, ld_sem.at[1])
    load_tiles.start()

    count = tcnt[0, 0]

    def chain(t, lasts):
        row = jnp.where(t < count, trow[0, 0, t], -1)
        before = jnp.int32(0)
        new = []
        for i in range(RB):
            hit = row == i
            before = jnp.where(hit, lasts[i], before)
            new.append(jnp.where(hit, t + 1, lasts[i]))
        prev[t] = before
        return tuple(new)

    lasts = lax.fori_loop(0, SLOTS, chain, tuple(jnp.int32(0) for _ in range(RB)))
    for i in range(RB):
        last[i] = lasts[i]
    run[0] = jnp.zeros((NY * RHS, TILE), jnp.float32)

    load_src.wait()
    stacked = jnp.concatenate([src[:, b * TILE : (b + 1) * TILE] for b in range(RB)], axis=0)
    coef = split_dot(stacked, st_ref[...]) * fac_ref[...]
    blocks = [coef[b * RHS : (b + 1) * RHS] for b in range(RB)]
    coarse = [blocks[b][:, :128] for b in range(RB)]
    stride = 1
    while stride < RB:
        for p in range(0, RB, 2 * stride):
            u, v = coarse[p], coarse[p + stride]
            coarse[p], coarse[p + stride] = (u + v) * ROOT_HALF, (u - v) * ROOT_HALF
        stride *= 2
    first = lax.broadcasted_iota(jnp.int32, (RHS, 128), 1) == 0
    for b in range(RB):
        low = jnp.where(first, coarse[b], blocks[b][:, :128])
        wav[b, :, :128] = low.astype(jnp.bfloat16)
        wav[b, :, 128:] = blocks[b][:, 128:].astype(jnp.bfloat16)
    fsend[...] = coarse[0]

    pl.semaphore_wait(bar, jnp.where(z == c, NROW - 1 + NCOL - 1 + NY, NROW - 1 + NCOL + NY))

    def f_copy(level, target):
        return pltpu.make_async_remote_copy(
            src_ref=fsend, dst_ref=frecv.at[r], send_sem=f_ss.at[level], recv_sem=f_rs.at[r],
            device_id=(target, c), device_id_type=MESH,
        )

    targets = [(r // 2 ** (lv + 1)) * 2 ** (lv + 1) + 2**lv for lv in range(LEVELS)] + [r * 0]
    for level in reversed(range(LEVELS + 1)):
        @pl.when(targets[level] != r)
        def _():
            f_copy(level, targets[level]).start()

    def half(ref, h):
        return ref.at[pl.ds(HALF - HALF * h, HALF)]

    def piece(ref, ys, xi, h):
        return ref.at[ys, pl.ds(xi * RB + HALF - HALF * h, HALF)]

    ORDER = (1, 7, 2, 6, 3, 5, 4, 0)

    def stage_a(h):
        for kk in range(NK):
            @pl.when(k == kk)
            def _():
                def send(j, carry):
                    zt = lax.rem(z + j, NZ)
                    copy = pltpu.make_async_remote_copy(
                        src_ref=half(wav, h), dst_ref=piece(xs[kk], y, x, h),
                        send_sem=a_ss.at[h * NZ + j], recv_sem=a_rs.at[(h * NK + kk) * NY + y],
                        device_id=(zt * NX + x, z), device_id_type=MESH,
                    )
                    copy.start()
                    return carry

                @pl.when(z != c)
                def _():
                    send(0, 0)

                @pl.when(z == c)
                def _():
                    pltpu.make_async_copy(half(wav, h), piece(xs[kk], y, x, h), l_sem.at[h]).start()

                for j in (4, 3, 5, 2, 6, 1, 7):
                    send(j, 0)

    def stage_a_done(h):
        for j in range(NZ):
            wait = pltpu.make_async_copy(half(wav, h), half(wav, h), a_ss.at[h * NZ + j])
            if j == 0:
                @pl.when(z != c)
                def _():
                    wait.wait()
            else:
                wait.wait()

    def b_copy(kk, ys, h, d):
        ref = xs[kk]
        i = ((h * NK + kk) * NY + ys) * 2 + d
        to = lax.rem(x + 1 + 2 * d, NX)
        return pltpu.make_async_remote_copy(
            src_ref=piece(ref, ys, x, h), dst_ref=piece(ref, ys, x, h),
            send_sem=b_ss.at[i], recv_sem=b_rs.at[i],
            device_id=(z * NX + to, c), device_id_type=MESH,
        )

    def r_copy(kk, ys, h, d):
        ref = xs[kk]
        i = (h * NK + kk) * NY + ys
        to = lax.rem(x + 1 + 2 * d, NX)
        origin = lax.rem(x + 3 - 2 * d, NX)
        return pltpu.make_async_remote_copy(
            src_ref=piece(ref, ys, origin, h), dst_ref=piece(ref, ys, origin, h),
            send_sem=r_ss.at[i], recv_sem=r_rs.at[i],
            device_id=(z * NX + to, c), device_id_type=MESH,
        )

    def wait_for(ref, sem):
        pltpu.make_async_copy(ref, ref, sem).wait()

    def b_arrived(kk, ys, h, d):
        i = ((h * NK + kk) * NY + ys) * 2 + d
        wait_for(piece(xs[kk], ys, lax.rem(x + 3 - 2 * d, NX), h), b_rs.at[i])

    def r_arrived(kk, ys, h):
        i = (h * NK + kk) * NY + ys
        wait_for(piece(xs[kk], ys, lax.rem(x + 2, NX), h), r_rs.at[i])

    def serve(kk, h):
        for ys in range(NY):
            i = (h * NK + kk) * NY + ys
            mine = piece(xs[kk], ys, x, h)
            local = jnp.logical_and(z == c, c == ys * NK + kk)

            @pl.when(local)
            def _():
                pltpu.make_async_copy(mine, mine, l_sem.at[h]).wait()

            @pl.when(jnp.logical_not(local))
            def _():
                pltpu.make_async_copy(mine, mine, a_rs.at[i]).wait()

            b_copy(kk, ys, h, 0).start()
            b_copy(kk, ys, h, 1).start()

    def relay(kk, h):
        for ys in range(NY):
            d = (ys + h) % 2
            b_arrived(kk, ys, h, d)
            r_copy(kk, ys, h, d).start()

    def finish(kk, h):
        for ys in range(NY):
            d = (ys + h) % 2
            b_arrived(kk, ys, h, 1 - d)
            r_arrived(kk, ys, h)

    def sends_done(kk, h):
        for ys in range(NY):
            b_copy(kk, ys, h, 0).wait_send()
            b_copy(kk, ys, h, 1).wait_send()
            r_copy(kk, ys, h, (ys + h) % 2).wait_send()

    stage_a(0)
    serve(0, 0)

    for level in range(LEVELS + 1):
        size = 2 ** (level + 1) if level < LEVELS else NROW
        mine = (lax.rem(r, size) == 2**level) if level < LEVELS else (r == 0)

        @pl.when(mine)
        def _():
            base = (r // size) * size

            def arrive(j, carry):
                sender = base + j

                @pl.when(sender != r)
                def _():
                    pltpu.make_async_copy(fsend, frecv.at[sender], f_rs.at[sender]).wait()

                @pl.when(sender == r)
                def _():
                    frecv[r] = fsend[...]

                return carry

            lax.fori_loop(0, size, arrive, 0)
            total = jnp.zeros((RHS, 128), jnp.float32)
            for j in range(size):
                value = frecv[base + j]
                total = total - value if level < LEVELS and j >= size // 2 else total + value
            facc[...] = total * (size**-0.5)

    wav[0, :, :128] = jnp.where(first, facc[...], wav[0, :, :128].astype(jnp.float32)).astype(jnp.bfloat16)
    stage_a(1)
    serve(1, 0)
    relay(0, 0)
    serve(0, 1)
    relay(1, 0)
    finish(0, 0)
    serve(1, 1)
    relay(0, 1)
    relay(1, 1)
    finish(0, 1)
    load_tiles.wait()

    def compute(kk, lo, hi):
        ref = xs[kk]

        def step(t, carry):
            side = ref[:, pl.ds(tcol[0, 0, t], 1)].reshape(NY * RHS, TILE)
            product = jnp.dot(side, tiles[t], preferred_element_type=jnp.float32)
            run[t + 1] = run[prev[t]] + product
            return carry

        lax.fori_loop(lo, hi, step, 0, unroll=4)

    k_copy = pltpu.make_async_remote_copy(
        src_ref=part, dst_ref=recvk, send_sem=k_ss.at[0], recv_sem=k_rs.at[0],
        device_id=(r, y * NK + 1 - k), device_id_type=MESH,
    )

    def give(kk):
        @pl.when(k != kk)
        def _():
            for i in range(RB):
                part[i] = run[last[i]]
            k_copy.start()

    def y_copy(d):
        to = lax.rem(y + d, NY)
        return pltpu.make_async_remote_copy(
            src_ref=ysend.at[to], dst_ref=yrecv.at[d], send_sem=y_ss.at[d], recv_sem=y_rs.at[d],
            device_id=(r, to * NK + k), device_id_type=MESH,
        )

    def take(kk):
        @pl.when(k == kk)
        def _():
            k_copy.wait_recv()
            for i in range(RB):
                total = (run[last[i]] + recvk[i]).reshape(NY, RHS, TILE)
                psum[:, i] = total
                ysend[:, i] = total.astype(jnp.bfloat16)
            for d in (2, 1, 3):
                y_copy(d).start()

    compute(0, 0, SLOTS)
    give(0)
    take(0)
    finish(1, 0)
    finish(1, 1)
    compute(1, 0, SLOTS)
    give(1)
    take(1)

    for d in (1, 3, 2):
        y_copy(d).wait_recv()
    for i in range(RB):
        total = psum[y, i]
        for d in range(1, NY):
            total = total + yrecv[d, i].astype(jnp.float32)
        image[i] = total
    tsend[...] = image[0, :, :128]

    def t_copy(slot, j, target):
        return pltpu.make_async_remote_copy(
            src_ref=tsend, dst_ref=trecv.at[slot], send_sem=t_ss.at[j], recv_sem=t_rs.at[slot],
            device_id=(target, c), device_id_type=MESH,
        )

    for level in range(LEVELS + 1):
        size = 2 ** (level + 1) if level < LEVELS else NROW
        mine = (lax.rem(r, size) == 2**level) if level < LEVELS else (r == 0)

        @pl.when(mine)
        def _():
            base = (r // size) * size

            def spread(j, carry):
                t_copy(level, j, base + lax.rem(r - base + j, size)).start()
                return carry

            lax.fori_loop(1, size, spread, 0)

    lane0 = lax.broadcasted_iota(jnp.int32, (RHS, TILE), 1) == 0
    plain = jnp.concatenate([jnp.where(lane0, 0.0, image[i]) for i in range(RB)], axis=0)
    result = split_dot(plain * fac_ref[...], s_ref[...])

    top = jnp.zeros((RHS, 128), jnp.float32)
    for level in range(LEVELS + 1):
        @pl.when(targets[level] != r)
        def _():
            pltpu.make_async_copy(tsend, trecv.at[level], t_rs.at[level]).wait()

        @pl.when(targets[level] == r)
        def _():
            trecv[level] = tsend[...]

    for level in range(LEVELS + 1):
        size = 2 ** (level + 1) if level < LEVELS else NROW
        weight = size**-0.5
        if level < LEVELS:
            weight = jnp.where(lax.rem(r, size) < size // 2, weight, -weight)
        top = top + trecv[level] * weight

    back = [top] + [image[i, :, :128] for i in range(1, RB)]
    stride = RB // 2
    while stride >= 1:
        for p in range(0, RB, 2 * stride):
            u, v = back[p], back[p + stride]
            back[p], back[p + stride] = (u + v) * ROOT_HALF, (u - v) * ROOT_HALF
        stride //= 2
    for b in range(RB):
        level0 = jnp.broadcast_to(back[b][:, :1] * (TILE**-0.5), (RHS, TILE))
        out_ref[:, b * TILE : (b + 1) * TILE] = result[b * RHS : (b + 1) * RHS] + level0

    for level in range(LEVELS + 1):
        @pl.when(targets[level] != r)
        def _():
            f_copy(level, targets[level]).wait_send()
    stage_a_done(0)
    stage_a_done(1)
    for h in range(2):
        for kk in range(NK):
            sends_done(kk, h)
    k_copy.wait_send()
    for d in range(1, NY):
        y_copy(d).wait_send()
    for level in range(LEVELS + 1):
        size = 2 ** (level + 1) if level < LEVELS else NROW
        mine = (lax.rem(r, size) == 2**level) if level < LEVELS else (r == 0)

        @pl.when(mine)
        def _():
            def sent(j, carry):
                pltpu.make_async_copy(tsend, tsend, t_ss.at[j]).wait()
                return carry

            lax.fori_loop(1, size, sent, 0)


def local(sources, tiles, tile_row, tile_col, tile_count):
    table, factor = sign_table(TILE)
    s_mat = jnp.asarray(table, jnp.bfloat16)
    st_mat = jnp.asarray(table.T.copy(), jnp.bfloat16)
    fac = jnp.asarray(factor[None, :], jnp.float32)
    vmem = pl.BlockSpec(memory_space=pltpu.VMEM)
    smem = pl.BlockSpec(memory_space=pltpu.SMEM)
    hbm = pl.BlockSpec(memory_space=pl.ANY)
    f32, b16 = jnp.float32, jnp.bfloat16
    dma = pltpu.SemaphoreType.DMA
    return pl.pallas_call(
        kernel,
        out_shape=jax.ShapeDtypeStruct((RHS, RB * TILE), f32),
        in_specs=[hbm, hbm, smem, smem, smem, vmem, vmem, vmem],
        out_specs=vmem,
        scratch_shapes=[
            pltpu.VMEM((RHS, RB * TILE), f32),
            pltpu.VMEM((SLOTS, TILE, TILE), b16),
            pltpu.VMEM((RB, RHS, TILE), b16),
            pltpu.VMEM((NY, NX * RB, RHS, TILE), b16),
            pltpu.VMEM((NY, NX * RB, RHS, TILE), b16),
            pltpu.VMEM((SLOTS + 1, NY * RHS, TILE), f32),
            pltpu.VMEM((RB, NY * RHS, TILE), f32),
            pltpu.VMEM((RB, NY * RHS, TILE), f32),
            pltpu.VMEM((NY, RB, RHS, TILE), f32),
            pltpu.VMEM((NY, RB, RHS, TILE), b16),
            pltpu.VMEM((NY, RB, RHS, TILE), b16),
            pltpu.VMEM((RB, RHS, TILE), f32),
            pltpu.VMEM((RHS, 128), f32),
            pltpu.VMEM((NROW, RHS, 128), f32),
            pltpu.VMEM((RHS, 128), f32),
            pltpu.VMEM((RHS, 128), f32),
            pltpu.VMEM((LEVELS + 1, RHS, 128), f32),
            pltpu.SMEM((SLOTS,), jnp.int32),
            pltpu.SMEM((RB,), jnp.int32),
            dma((2,)),
            dma((LEVELS + 1,)),
            dma((NROW,)),
            dma((2 * NZ,)),
            dma((2 * NCOL,)),
            dma((2,)),
            dma((4 * NCOL,)),
            dma((4 * NCOL,)),
            dma((2 * NCOL,)),
            dma((2 * NCOL,)),
            dma((1,)),
            dma((1,)),
            dma((NY,)),
            dma((NY,)),
            dma((NROW,)),
            dma((LEVELS + 1,)),
        ],
        compiler_params=pltpu.CompilerParams(
            collective_id=0, has_side_effects=True, vmem_limit_bytes=48 * 2**20
        ),
    )(sources, tiles, tile_row, tile_col, tile_count, st_mat, s_mat, fac)


def solution(mesh):
    return jax.shard_map(
        local,
        mesh=mesh,
        in_specs=(
            P("col", "row"),
            P("row", "col", None, None, None),
            P("row", "col", None),
            P("row", "col", None),
            P("row", "col"),
        ),
        out_specs=P("col", "row"),
        check_vma=False,
    )
```

time: 299 us -> 65.1 us (0.22)
  the two profiles are of different devices: /device:TPU:2 before, /device:TPU:1 now
where the time goes in v1:
time: 65.1 us; the launch traced here: 64.9 us
  Pallas kernels  58.9 us (90%)
  local copies, waits for them, and re-layouts  5.35 us (8%)
  between operations  0.67 us (1%)
    pallas_call x1, Pallas kernels, local(): pl.pallas_call(kernel, out_shape=jax.ShapeDtypeStruct((RHS, RB * TILE), f...  58.9 us
    unnamed x13, local copies, waits for them, and re-layouts  5.35 us

profile of v1, /device:TPU:1, one launch (start us, length us, event | category | flops | bytes accessed | tf_op | source)
XLA Modules:
  0.0 64.9 jit_solution(12112458309234150665)
XLA Ops:
  0.7 0.0 copy-start
  0.7 0.9 %copy-done = f32[16,2048]{1,0:T(8,128)S(1)} copy-done((f32[16,2048]{1,0:T(8,128)S(1)}, f32[16,2048]{1,0:T(8,128)}, u32[]{:S(2)}) %copy-start) | copy-done | bytes 131096
  1.6 0.0 copy-start.1
  1.6 0.9 %copy-done.1 = bf16[256,256]{1,0:T(8,128)(2,1)S(1)} copy-done((bf16[256,256]{1,0:T(8,128)(2,1)S(1)}, bf16[256,256]{1,0:T(8,128)(2,1)}, u32[]{:S(2)}) %copy-start.1) | copy-done | bytes 131096
  2.5 0.0 copy-start.2
  2.5 0.9 %copy-done.2 = bf16[256,256]{1,0:T(8,128)(2,1)S(1)} copy-done((bf16[256,256]{1,0:T(8,128)(2,1)S(1)}, bf16[256,256]{1,0:T(8,128)(2,1)}, u32[]{:S(2)}) %copy-start.2) | copy-done | bytes 131096
  3.4 0.0 copy-start.3
  3.4 0.7 %copy-done.3 = f32[1,256]{1,0:T(1,128)S(1)} copy-done((f32[1,256]{1,0:T(1,128)S(1)}, f32[1,256]{1,0:T(1,128)}, u32[]{:S(2)}) %copy-start.3) | copy-done | bytes 1048
  4.0 0.0 copy-start.4
  4.0 0.7 %copy-done.4 = s32[1,1,48]{2,1,0:T(1,128)S(1)} copy-done((s32[1,1,48]{2,1,0:T(1,128)S(1)}, s32[1,1,48]{2,1,0:T(1,128)}, u32[]{:S(2)}) %copy-start.4) | copy-done | bytes 216
  4.7 0.0 copy-start.5
  4.7 0.7 %copy-done.5 = s32[1,1,48]{2,1,0:T(1,128)S(1)} copy-done((s32[1,1,48]{2,1,0:T(1,128)S(1)}, s32[1,1,48]{2,1,0:T(1,128)}, u32[]{:S(2)}) %copy-start.5) | copy-done | bytes 216
  5.4 58.9 %shard_map.82 = f32[16,2048]{1,0:T(8,128)S(1)} custom-call(f32[16,2048]{1,0:T(8,128)S(1)} %copy-done, bf16[1,1,48,256,256]{4,3,2,1,0:T(8,128)(2,1)} %tiles_hbm.1, s32[1,1,48]{2,1,0:T(1,128)S(1)} %copy-done.4, s32[1,1,48]{2,1,0:T(1,128)S(1)} %copy-done.5, s32[1,1]{1,0:T(1,128)S(6)} %copy.10.tcnt, bf16[256,256]{1,0:T(8,128)(2,1)S(1)} %copy-done.1, ...), custom_call_target="tpu_custom_call" | custom-call | tf_op jit(solution)/shard_map/pallas_call | solution.py:435
  64.2 0.7 %copy.11 = f32[16,2048]{1,0:T(8,128)} copy(f32[16,2048]{1,0:T(8,128)S(1)} %shard_map.82) | data formatting | bytes 262144
Async XLA Ops:
  0.7 0.9 %copy-start = (f32[16,2048]{1,0:T(8,128)S(1)}, f32[16,2048]{1,0:T(8,128)}, u32[]{:S(2)}) copy-start(f32[16,2048]{1,0:T(8,128)} %src_hbm.1) | copy-start | bytes 393220
  1.6 0.9 %copy-start.1 = (bf16[256,256]{1,0:T(8,128)(2,1)S(1)}, bf16[256,256]{1,0:T(8,128)(2,1)}, u32[]{:S(2)}) copy-start(bf16[256,256]{1,0:T(8,128)(2,1)} %constant.7.clone.st_ref) | copy-start | bytes 393220
  2.5 0.9 %copy-start.2 = (bf16[256,256]{1,0:T(8,128)(2,1)S(1)}, bf16[256,256]{1,0:T(8,128)(2,1)}, u32[]{:S(2)}) copy-start(bf16[256,256]{1,0:T(8,128)(2,1)} %constant.6.clone.s_ref) | copy-start | bytes 393220
  3.4 0.7 %copy-start.3 = (f32[1,256]{1,0:T(1,128)S(1)}, f32[1,256]{1,0:T(1,128)}, u32[]{:S(2)}) copy-start(f32[1,256]{1,0:T(1,128)} %constant.8.clone.fac_ref) | copy-start | bytes 3076
  4.0 0.7 %copy-start.4 = (s32[1,1,48]{2,1,0:T(1,128)S(1)}, s32[1,1,48]{2,1,0:T(1,128)}, u32[]{:S(2)}) copy-start(s32[1,1,48]{2,1,0:T(1,128)} %trow.1) | copy-start | bytes 580
  4.7 0.7 %copy-start.5 = (s32[1,1,48]{2,1,0:T(1,128)S(1)}, s32[1,1,48]{2,1,0:T(1,128)}, u32[]{:S(2)}) copy-start(s32[1,1,48]{2,1,0:T(1,128)} %tcol.1) | copy-start | bytes 580

commit v2 on v1

--- a/solution.py
+++ b/solution.py
@@ -45,8 +45,9 @@
 
 
 def kernel(
-    src_hbm, tiles_hbm, trow, tcol, tcnt, st_ref, s_ref, fac_ref,
+    src_hbm, tiles_hbm, trow_hbm, tcol_hbm, tcnt_hbm, st_hbm, s_hbm, fac_hbm,
     out_ref,
+    trow, tcol, tcnt, st_ref, s_ref, fac_ref,
     src, tiles, wav, xa, xb, run, part, recvk, psum, ysend, yrecv, image,
     fsend, frecv, facc, tsend, trecv, prev, last,
     ld_sem, f_ss, f_rs, a_ss, a_rs, l_sem, b_ss, b_rs, r_ss, r_rs, k_ss, k_rs, y_ss, y_rs, t_ss, t_rs,
@@ -77,10 +78,15 @@
     for d in range(1, NY):
         pl.semaphore_signal(bar, inc=1, device_id=(r, lax.rem(y + d, NY) * NK + k), device_id_type=MESH)
 
-    load_src = pltpu.make_async_copy(src_hbm, src, ld_sem.at[0])
-    load_src.start()
-    load_tiles = pltpu.make_async_copy(tiles_hbm.at[0, 0], tiles, ld_sem.at[1])
-    load_tiles.start()
+    pairs = (
+        (trow_hbm, trow), (tcol_hbm, tcol), (tcnt_hbm, tcnt), (src_hbm, src), (st_hbm, st_ref), (fac_hbm, fac_ref),
+        (s_hbm, s_ref), (tiles_hbm.at[0, 0], tiles),
+    )
+    loads = [pltpu.make_async_copy(a, b, ld_sem.at[i]) for i, (a, b) in enumerate(pairs)]
+    for load in loads:
+        load.start()
+    for load in loads[:3]:
+        load.wait()
 
     count = tcnt[0, 0]
 
@@ -100,7 +106,8 @@
         last[i] = lasts[i]
     run[0] = jnp.zeros((NY * RHS, TILE), jnp.float32)
 
-    load_src.wait()
+    for load in loads[3:6]:
+        load.wait()
     stacked = jnp.concatenate([src[:, b * TILE : (b + 1) * TILE] for b in range(RB)], axis=0)
     coef = split_dot(stacked, st_ref[...]) * fac_ref[...]
     blocks = [coef[b * RHS : (b + 1) * RHS] for b in range(RB)]
@@ -138,42 +145,39 @@
     def piece(ref, ys, xi, h):
         return ref.at[ys, pl.ds(xi * RB + HALF - HALF * h, HALF)]
 
-    ORDER = (1, 7, 2, 6, 3, 5, 4, 0)
-
     def stage_a(h):
         for kk in range(NK):
             @pl.when(k == kk)
             def _():
                 def send(j, carry):
-                    zt = lax.rem(z + j, NZ)
-                    copy = pltpu.make_async_remote_copy(
-                        src_ref=half(wav, h), dst_ref=piece(xs[kk], y, x, h),
-                        send_sem=a_ss.at[h * NZ + j], recv_sem=a_rs.at[(h * NK + kk) * NY + y],
-                        device_id=(zt * NX + x, z), device_id_type=MESH,
-                    )
-                    copy.start()
+                    dz = lax.rem(NK * y + kk + j, NZ)
+                    to = lax.rem(z + dz, NZ)
+                    mine = jnp.logical_and(dz == 0, z == c)
+
+                    @pl.when(jnp.logical_not(mine))
+                    def _():
+                        pltpu.make_async_remote_copy(
+                            src_ref=half(wav, h), dst_ref=piece(xs[kk], y, x, h),
+                            send_sem=a_ss.at[h * NZ + j], recv_sem=a_rs.at[(h * NK + kk) * NY + y],
+                            device_id=(to * NX + x, z), device_id_type=MESH,
+                        ).start()
+
+                    @pl.when(mine)
+                    def _():
+                        pltpu.make_async_copy(half(wav, h), piece(xs[kk], y, x, h), l_sem.at[h]).start()
+
                     return carry
 
-                @pl.when(z != c)
-                def _():
-                    send(0, 0)
-
-                @pl.when(z == c)
-                def _():
-                    pltpu.make_async_copy(half(wav, h), piece(xs[kk], y, x, h), l_sem.at[h]).start()
-
-                for j in (4, 3, 5, 2, 6, 1, 7):
-                    send(j, 0)
+                lax.fori_loop(0, NZ, send, 0)
 
     def stage_a_done(h):
         for j in range(NZ):
-            wait = pltpu.make_async_copy(half(wav, h), half(wav, h), a_ss.at[h * NZ + j])
-            if j == 0:
-                @pl.when(z != c)
-                def _():
-                    wait.wait()
-            else:
-                wait.wait()
+            @pl.when(jnp.logical_not(jnp.logical_and(lax.rem(NK * y + k + j, NZ) == 0, z == c)))
+            def _():
+                pltpu.make_async_copy(half(wav, h), half(wav, h), a_ss.at[h * NZ + j]).wait()
+
+    def source(kk, m):
+        return lax.rem(lax.rem(z - c + 2 * NZ - kk, NZ) // 2 - m + NY, NY)
 
     def b_copy(kk, ys, h, d):
         ref = xs[kk]
@@ -207,43 +211,46 @@
         i = (h * NK + kk) * NY + ys
         wait_for(piece(xs[kk], ys, lax.rem(x + 2, NX), h), r_rs.at[i])
 
-    def serve(kk, h):
-        for ys in range(NY):
-            i = (h * NK + kk) * NY + ys
-            mine = piece(xs[kk], ys, x, h)
-            local = jnp.logical_and(z == c, c == ys * NK + kk)
-
-            @pl.when(local)
-            def _():
-                pltpu.make_async_copy(mine, mine, l_sem.at[h]).wait()
-
-            @pl.when(jnp.logical_not(local))
-            def _():
-                pltpu.make_async_copy(mine, mine, a_rs.at[i]).wait()
-
-            b_copy(kk, ys, h, 0).start()
-            b_copy(kk, ys, h, 1).start()
-
-    def relay(kk, h):
-        for ys in range(NY):
-            d = (ys + h) % 2
-            b_arrived(kk, ys, h, d)
-            r_copy(kk, ys, h, d).start()
+    def serve(kk, h, m):
+        ys = source(kk, m)
+        i = (h * NK + kk) * NY + ys
+        mine = piece(xs[kk], ys, x, h)
+        local = jnp.logical_and(z == c, c == ys * NK + kk)
+
+        @pl.when(local)
+        def _():
+            wait_for(mine, l_sem.at[h])
+
+        @pl.when(jnp.logical_not(local))
+        def _():
+            wait_for(mine, a_rs.at[i])
+
+        b_copy(kk, ys, h, 0).start()
+        b_copy(kk, ys, h, 1).start()
+
+    def relay(kk, h, m):
+        ys = source(kk, m)
+        d = (m + h) % 2
+        b_arrived(kk, ys, h, d)
+        r_copy(kk, ys, h, d).start()
 
     def finish(kk, h):
-        for ys in range(NY):
-            d = (ys + h) % 2
-            b_arrived(kk, ys, h, 1 - d)
+        for m in range(NY):
+            ys = source(kk, m)
+            b_arrived(kk, ys, h, 1 - (m + h) % 2)
             r_arrived(kk, ys, h)
 
     def sends_done(kk, h):
-        for ys in range(NY):
+        for m in range(NY):
+            ys = source(kk, m)
             b_copy(kk, ys, h, 0).wait_send()
             b_copy(kk, ys, h, 1).wait_send()
-            r_copy(kk, ys, h, (ys + h) % 2).wait_send()
+            r_copy(kk, ys, h, (m + h) % 2).wait_send()
 
     stage_a(0)
-    serve(0, 0)
+    for m in range(2):
+        serve(0, 0, m)
+        serve(1, 0, m)
 
     for level in range(LEVELS + 1):
         size = 2 ** (level + 1) if level < LEVELS else NROW
@@ -274,17 +281,39 @@
             facc[...] = total * (size**-0.5)
 
     wav[0, :, :128] = jnp.where(first, facc[...], wav[0, :, :128].astype(jnp.float32)).astype(jnp.bfloat16)
-    stage_a(1)
-    serve(1, 0)
-    relay(0, 0)
-    serve(0, 1)
-    relay(1, 0)
+    @pl.when(k == 0)
+    def _():
+        stage_a(1)
+
+    for m in range(2, NY):
+        serve(0, 0, m)
+        relay(0, 0, m - 2)
+        serve(1, 0, m)
+        relay(1, 0, m - 2)
+
+    @pl.when(k == 1)
+    def _():
+        stage_a(1)
+
+    for m in range(NY):
+        serve(0, 1, m)
+        if m < 2:
+            relay(0, 0, m + 2)
+            relay(1, 0, m + 2)
+        else:
+            relay(0, 1, m - 2)
+    for m in range(NY):
+        serve(1, 1, m)
+        if m < 2:
+            relay(0, 1, m + 2)
+        else:
+            relay(1, 1, m - 2)
+    relay(1, 1, 2)
+    relay(1, 1, 3)
     finish(0, 0)
-    serve(1, 1)
-    relay(0, 1)
-    relay(1, 1)
     finish(0, 1)
-    load_tiles.wait()
+    loads[6].wait()
+    loads[7].wait()
 
     def compute(kk, lo, hi):
         ref = xs[kk]
@@ -428,16 +457,21 @@
     st_mat = jnp.asarray(table.T.copy(), jnp.bfloat16)
     fac = jnp.asarray(factor[None, :], jnp.float32)
     vmem = pl.BlockSpec(memory_space=pltpu.VMEM)
-    smem = pl.BlockSpec(memory_space=pltpu.SMEM)
-    hbm = pl.BlockSpec(memory_space=pl.ANY)
+    hbm = pl.BlockSpec(memory_space=pltpu.HBM)
     f32, b16 = jnp.float32, jnp.bfloat16
     dma = pltpu.SemaphoreType.DMA
     return pl.pallas_call(
         kernel,
         out_shape=jax.ShapeDtypeStruct((RHS, RB * TILE), f32),
-        in_specs=[hbm, hbm, smem, smem, smem, vmem, vmem, vmem],
+        in_specs=[hbm] * 8,
         out_specs=vmem,
         scratch_shapes=[
+            pltpu.SMEM((1, 1, SLOTS), jnp.int32),
+            pltpu.SMEM((1, 1, SLOTS), jnp.int32),
+            pltpu.SMEM((1, 1), jnp.int32),
+            pltpu.VMEM((TILE, TILE), b16),
+            pltpu.VMEM((TILE, TILE), b16),
+            pltpu.VMEM((1, TILE), f32),
             pltpu.VMEM((RHS, RB * TILE), f32),
             pltpu.VMEM((SLOTS, TILE, TILE), b16),
             pltpu.VMEM((RB, RHS, TILE), b16),
@@ -457,7 +491,7 @@
             pltpu.VMEM((LEVELS + 1, RHS, 128), f32),
             pltpu.SMEM((SLOTS,), jnp.int32),
             pltpu.SMEM((RB,), jnp.int32),
-            dma((2,)),
+            dma((8,)),
             dma((LEVELS + 1,)),
             dma((NROW,)),
             dma((2 * NZ,)),
@@ -475,7 +509,7 @@
             dma((LEVELS + 1,)),
         ],
         compiler_params=pltpu.CompilerParams(
-            collective_id=0, has_side_effects=True, vmem_limit_bytes=48 * 2**20
+            collective_id=0, has_side_effects=True, vmem_limit_bytes=64 * 2**20
         ),
     )(sources, tiles, tile_row, tile_col, tile_count, st_mat, s_mat, fac)
 

time: 65.1 us -> 61.7 us (0.948)
  local copies, waits for them, and re-layouts: 5.35 us -> 1.57 us
    unnamed x13 -> x1, local copies, waits for them, and re-layouts: 5.35 us -> 1.57 us
where the time goes in v2:
time: 61.7 us; the launch traced here: 61.6 us
  Pallas kernels  59.4 us (96%)
  local copies, waits for them, and re-layouts  1.57 us (3%)
  between operations  0.66 us (1%)
    pallas_call x1, Pallas kernels, local(): pl.pallas_call(kernel, out_shape=jax.ShapeDtypeStruct((RHS, RB * TILE), f...  59.4 us
    unnamed x1, local copies, waits for them, and re-layouts  1.57 us

profile of v2, /device:TPU:1, one launch (start us, length us, event | category | flops | bytes accessed | tf_op | source)
XLA Modules:
  0.0 61.6 jit_solution(13060507937372159976)
XLA Ops:
  0.7 59.4 %shard_map.82 = f32[16,2048]{1,0:T(8,128)} custom-call(f32[16,2048]{1,0:T(8,128)} %src_hbm.1, bf16[1,1,48,256,256]{4,3,2,1,0:T(8,128)(2,1)} %tiles_hbm.1, s32[1,1,48]{2,1,0:T(1,128)} %trow_hbm.1, s32[1,1,48]{2,1,0:T(1,128)} %tcol_hbm.1, s32[1,1]{1,0:T(1,128)S(6)} %copy.10.tcnt_hbm, bf16[256,256]{1,0:T(8,128)(2,1)} %constant.7.clone.st_hbm, ...), custom_call_target="tpu_custom_call" | custom-call | tf_op jit(solution)/shard_map/pallas_call | solution.py:463
  60.0 1.6 %copy.11 = f32[16,2048]{1,0:T(8,128)} copy(f32[16,2048]{1,0:T(8,128)} %shard_map.82) | data formatting | bytes 262144

commit v3 on v2

v3 whole, which is shorter than its diff:
```python
import math

import jax
import jax.numpy as jnp
import numpy as np
from jax import lax
from jax.experimental import pallas as pl
from jax.experimental.pallas import tpu as pltpu
from jax.sharding import PartitionSpec as P

MESH = pl.DeviceIdType.MESH
ROOT_HALF = 1.0 / math.sqrt(2.0)
NX, NY, NZ, NK = 4, 4, 8, 2
NROW, NCOL = NX * NZ, NY * NK
TILE = 256
RHS = 16
RB = 8
SLOTS = 48
PARTS = ((4, 4), (0, 4))
NPART = len(PARTS)
LAG = 8
BEFORE = 2
MIDDLE = 6


def direct(m, h):
    return h == NPART - 1 and m >= NCOL - 1


LEVELS = 5


def sign_table(extent):
    signs = np.zeros((extent, extent), np.float32)
    factor = np.zeros((extent,), np.float64)
    signs[0] = 1.0
    factor[0] = extent**-0.5
    for n in range(1, extent):
        low = n & -n
        signs[n, n - low : n] = 1.0
        signs[n, n : n + low] = -1.0
        factor[n] = (2.0 * low) ** -0.5
    return signs, factor.astype(np.float32)


def split_dot(values, matrix):
    m = values.shape[0]
    hi = values.astype(jnp.bfloat16)
    rest = values - hi.astype(jnp.float32)
    mid = rest.astype(jnp.bfloat16)
    low = (rest - mid.astype(jnp.float32)).astype(jnp.bfloat16)
    stacked = jnp.concatenate([hi, mid, low], axis=0)
    out = jnp.dot(stacked, matrix, preferred_element_type=jnp.float32)
    return out[:m] + (out[m : 2 * m] + out[2 * m :])


def kernel(
    src_hbm, tiles_hbm, trow_hbm, tcol_hbm, tcnt_hbm, st_hbm, s_hbm, fac_hbm,
    out_ref,
    trow, tcol, tcnt, trow_v, tcol_v, st_ref, s_ref, fac_ref,
    src, tiles, wav, xa, run, part, recvk, ysend, yrecv, image,
    fsend, frecv, facc, tsend, trecv, column, upart, urecv, prev, last,
    ld_sem, f_ss, f_rs, a_ss, a_rs, l_sem, b_ss, b_rs, r_ss, r_rs, k_ss, k_rs, y_ss, y_rs, t_ss, t_rs, u_ss, u_rs,
):
    r = lax.axis_index("row")
    c = lax.axis_index("col")
    x, z = lax.rem(r, NX), r // NX
    y, k = c // NK, lax.rem(c, NK)

    bar = pltpu.get_barrier_semaphore()

    def signal_row(j, carry):
        pl.semaphore_signal(bar, inc=1, device_id=(lax.rem(r + j, NROW), c), device_id_type=MESH)
        return carry

    lax.fori_loop(1, NROW, signal_row, 0)

    def signal_source(j, carry):
        @pl.when(jnp.logical_not(jnp.logical_and(z == c, j == c)))
        def _():
            pl.semaphore_signal(bar, inc=1, device_id=(c * NX + x, j), device_id_type=MESH)

        return carry

    lax.fori_loop(0, NCOL, signal_source, 0)
    for d in range(1, NCOL):
        pl.semaphore_signal(bar, inc=1, device_id=(r, lax.rem(c + d, NCOL)), device_id_type=MESH)

    pairs = (
        (trow_hbm, trow), (tcol_hbm, tcol), (tcnt_hbm, tcnt), (src_hbm, src), (st_hbm, st_ref), (fac_hbm, fac_ref),
        (s_hbm, s_ref), (tiles_hbm.at[0, 0], tiles), (trow_hbm, trow_v), (tcol_hbm, tcol_v),
    )
    loads = [pltpu.make_async_copy(a, b, ld_sem.at[i]) for i, (a, b) in enumerate(pairs)]
    for load in loads:
        load.start()
    for load in loads[:3]:
        load.wait()

    count = tcnt[0, 0]

    def chain(t, lasts):
        row = jnp.where(t < count, trow[0, 0, t], -1)
        before = jnp.int32(0)
        new = []
        for i in range(RB):
            hit = row == i
            before = jnp.where(hit, lasts[i], before)
            new.append(jnp.where(hit, t + 1, lasts[i]))
        prev[t] = before
        return tuple(new)

    lasts = lax.fori_loop(0, SLOTS, chain, tuple(jnp.int32(0) for _ in range(RB)))
    for i in range(RB):
        last[i] = lasts[i]
    run[0] = jnp.zeros((NCOL, RHS, TILE), jnp.float32)

    for load in loads[3:6]:
        load.wait()
    stacked = jnp.concatenate([src[:, b * TILE : (b + 1) * TILE] for b in range(RB)], axis=0)
    coef = split_dot(stacked, st_ref[...]) * fac_ref[...]
    blocks = [coef[b * RHS : (b + 1) * RHS] for b in range(RB)]
    coarse = [blocks[b][:, :128] for b in range(RB)]
    stride = 1
    while stride < RB:
        for p in range(0, RB, 2 * stride):
            u, v = coarse[p], coarse[p + stride]
            coarse[p], coarse[p + stride] = (u + v) * ROOT_HALF, (u - v) * ROOT_HALF
        stride *= 2
    first = lax.broadcasted_iota(jnp.int32, (RHS, 128), 1) == 0
    for b in range(RB):
        low = jnp.where(first, coarse[b], blocks[b][:, :128])
        wav[b, :, :128] = low.astype(jnp.bfloat16)
        wav[b, :, 128:] = blocks[b][:, 128:].astype(jnp.bfloat16)
    fsend[...] = coarse[0]

    pl.semaphore_wait(bar, NROW - 1 + NCOL - 1 + NCOL - jnp.where(z == c, 1, 0))

    def f_copy(level, target):
        return pltpu.make_async_remote_copy(
            src_ref=fsend, dst_ref=frecv.at[r], send_sem=f_ss.at[level], recv_sem=f_rs.at[r],
            device_id=(target, c), device_id_type=MESH,
        )

    targets = [(r // 2 ** (lv + 1)) * 2 ** (lv + 1) + 2**lv for lv in range(LEVELS)] + [r * 0]
    for level in reversed(range(LEVELS + 1)):
        @pl.when(targets[level] != r)
        def _():
            f_copy(level, targets[level]).start()

    def half(ref, h):
        return ref.at[pl.ds(PARTS[h][0], PARTS[h][1])]

    def piece(cs, xi, h):
        return xa.at[cs, pl.ds(xi * RB + PARTS[h][0], PARTS[h][1])]

    def wait_for(ref, sem):
        pltpu.make_async_copy(ref, ref, sem).wait()

    def stage_a(h):
        def send(j, carry):
            dz = lax.rem(c + j, NZ)
            to = lax.rem(z + dz, NZ)
            mine = jnp.logical_and(dz == 0, z == c)

            @pl.when(jnp.logical_not(mine))
            def _():
                pltpu.make_async_remote_copy(
                    src_ref=half(wav, h), dst_ref=piece(c, x, h),
                    send_sem=a_ss.at[h * NZ + j], recv_sem=a_rs.at[h * NCOL + c],
                    device_id=(to * NX + x, z), device_id_type=MESH,
                ).start()

            @pl.when(mine)
            def _():
                pltpu.make_async_copy(half(wav, h), piece(c, x, h), l_sem.at[h]).start()

            return carry

        lax.fori_loop(0, NZ, send, 0)

    def stage_a_done(h):
        for j in range(NZ):
            @pl.when(jnp.logical_not(jnp.logical_and(lax.rem(c + j, NZ) == 0, z == c)))
            def _():
                wait_for(half(wav, h), a_ss.at[h * NZ + j])

    def source(m):
        return lax.rem(z - c - m + 3 * NZ, NCOL)

    def b_copy(m, h, d):
        cs = source(m)
        i = (h * NCOL + cs) * 2 + d
        to = lax.rem(x + 1 + 2 * d, NX)
        return pltpu.make_async_remote_copy(
            src_ref=piece(cs, x, h), dst_ref=piece(cs, x, h), send_sem=b_ss.at[i], recv_sem=b_rs.at[i],
            device_id=(z * NX + to, c), device_id_type=MESH,
        )

    def r_copy(m, h):
        cs = source(m)
        i = h * NCOL + cs
        d = (m + h) % 2
        if direct(m, h):
            origin, to = x, lax.rem(x + 2, NX)
        else:
            origin, to = lax.rem(x + 3 - 2 * d, NX), lax.rem(x + 1 + 2 * d, NX)
        return pltpu.make_async_remote_copy(
            src_ref=piece(cs, origin, h), dst_ref=piece(cs, origin, h), send_sem=r_ss.at[i], recv_sem=r_rs.at[i],
            device_id=(z * NX + to, c), device_id_type=MESH,
        )

    def b_arrived(m, h, d):
        cs = source(m)
        wait_for(piece(cs, lax.rem(x + 3 - 2 * d, NX), h), b_rs.at[(h * NCOL + cs) * 2 + d])

    def serve(m, h):
        cs = source(m)
        local = jnp.logical_and(z == c, c == cs)

        @pl.when(local)
        def _():
            wait_for(piece(cs, x, h), l_sem.at[h])

        @pl.when(jnp.logical_not(local))
        def _():
            wait_for(piece(cs, x, h), a_rs.at[h * NCOL + cs])

        b_copy(m, h, 0).start()
        b_copy(m, h, 1).start()
        if direct(m, h):
            r_copy(m, h).start()

    def relay(m, h):
        if not direct(m, h):
            b_arrived(m, h, (m + h) % 2)
            r_copy(m, h).start()

    def finish(m, h):
        cs = source(m)
        if direct(m, h):
            b_arrived(m, h, (m + h) % 2)
        b_arrived(m, h, 1 - (m + h) % 2)
        wait_for(piece(cs, lax.rem(x + 2, NX), h), r_rs.at[h * NCOL + cs])

    def sends_done(m, h):
        b_copy(m, h, 0).wait_send()
        b_copy(m, h, 1).wait_send()
        r_copy(m, h).wait_send()

    order = [(m, h) for h in range(NPART) for m in range(NCOL)]

    def serve_range(lo, hi):
        for n in range(lo, hi):
            if n < len(order):
                serve(*order[n])
            if 0 <= n - LAG:
                relay(*order[n - LAG])

    for h in range(NPART - 1):
        stage_a(h)
    serve_range(0, BEFORE)

    for level in range(LEVELS + 1):
        size = 2 ** (level + 1) if level < LEVELS else NROW
        mine = (lax.rem(r, size) == 2**level) if level < LEVELS else (r == 0)

        @pl.when(mine)
        def _():
            base = (r // size) * size

            def arrive(j, carry):
                sender = base + j

                @pl.when(sender != r)
                def _():
                    pltpu.make_async_copy(fsend, frecv.at[sender], f_rs.at[sender]).wait()

                @pl.when(sender == r)
                def _():
                    frecv[r] = fsend[...]

                return carry

            lax.fori_loop(0, size, arrive, 0)
            total = jnp.zeros((RHS, 128), jnp.float32)
            for j in range(size):
                value = frecv[base + j]
                total = total - value if level < LEVELS and j >= size // 2 else total + value
            facc[...] = total * (size**-0.5)

    wav[0, :, :128] = jnp.where(first, facc[...], wav[0, :, :128].astype(jnp.float32)).astype(jnp.bfloat16)
    stage_a(NPART - 1)
    serve_range(BEFORE, MIDDLE)

    for load in loads[6:]:
        load.wait()
    slot_lane = lax.broadcasted_iota(jnp.int32, (TILE, 128), 1)

    def pick(t, found):
        value = tiles[t, :, :128].astype(jnp.float32)
        return jnp.where(slot_lane == t, jnp.broadcast_to(value[:, :1], (TILE, 128)), found)

    found = lax.fori_loop(0, SLOTS, pick, jnp.zeros((TILE, 128), jnp.float32))
    slot = lax.broadcasted_iota(jnp.int32, (NX * RB, SLOTS), 1)
    block = lax.broadcasted_iota(jnp.int32, (NX * RB, SLOTS), 0)
    hit = (tcol_v[0] == block) & (trow_v[0] == 0) & (slot < count)
    column[...] = lax.dot_general(
        hit.astype(jnp.bfloat16), found[:, :SLOTS].astype(jnp.bfloat16), (((1,), (1,)), ((), ())),
        preferred_element_type=jnp.float32,
    )

    serve_range(MIDDLE, len(order) + LAG)
    for m, h in order:
        finish(m, h)

    def compute():
        def step(t, carry):
            side = xa[:, pl.ds(tcol[0, 0, t], 1)].reshape(NCOL * RHS, TILE)
            product = jnp.dot(side, tiles[t], preferred_element_type=jnp.float32)
            run[t + 1] = run[prev[t]] + product.reshape(NCOL, RHS, TILE)
            return carry

        lax.fori_loop(0, SLOTS, step, 0, unroll=16)

    def k_copy(d):
        return pltpu.make_async_remote_copy(
            src_ref=part.at[d], dst_ref=recvk.at[d], send_sem=k_ss.at[d], recv_sem=k_rs.at[d],
            device_id=(r, y * NK + 1 - k), device_id_type=MESH,
        )

    def y_copy(d):
        to = lax.rem(y + d, NY)
        return pltpu.make_async_remote_copy(
            src_ref=ysend.at[d], dst_ref=yrecv.at[d], send_sem=y_ss.at[d], recv_sem=y_rs.at[d],
            device_id=(r, to * NK + k), device_id_type=MESH,
        )

    def swap():
        for d in (2, 1, 3, 0):
            for i in range(RB):
                part[d, i] = run[last[i], lax.rem(y + d, NY) * NK + 1 - k]
            k_copy(d).start()

    def share():
        for d in (2, 1, 3, 0):
            k_copy(d).wait_recv()
            for i in range(RB):
                total = run[last[i], lax.rem(y + d, NY) * NK + k] + recvk[d, i]
                if d:
                    ysend[d, i] = total.astype(jnp.bfloat16)
                else:
                    image[i] = total
            if d:
                y_copy(d).start()

    def u_copy(d):
        to = lax.rem(c + d, NCOL)
        return pltpu.make_async_remote_copy(
            src_ref=upart.at[to], dst_ref=urecv.at[c], send_sem=u_ss.at[d], recv_sem=u_rs.at[c],
            device_id=(r, to), device_id_type=MESH,
        )

    def tops():
        def add(b, total):
            side = xa[:, pl.ds(b, 1)].reshape(NCOL * RHS, TILE).astype(jnp.float32)
            return total + side * column[pl.ds(b, 1), :]

        total = lax.fori_loop(0, NX * RB, add, jnp.zeros((NCOL * RHS, TILE), jnp.float32), unroll=4)
        value = jnp.sum(total, axis=1, keepdims=True)
        upart[...] = jnp.broadcast_to(value, (NCOL * RHS, 128)).reshape(NCOL, RHS, 128)
        for d in (4, 5, 3, 6, 2, 7, 1):
            u_copy(d).start()

    def t_copy(slot, j, target):
        return pltpu.make_async_remote_copy(
            src_ref=tsend, dst_ref=trecv.at[slot], send_sem=t_ss.at[j], recv_sem=t_rs.at[slot],
            device_id=(target, c), device_id_type=MESH,
        )

    def spread_tops():
        urecv[c] = upart[c]
        for d in range(1, NCOL):
            sender = lax.rem(c + d, NCOL)
            wait_for(urecv.at[sender], u_rs.at[sender])
        total = urecv[0]
        for sender in range(1, NCOL):
            total = total + urecv[sender]
        tsend[...] = total
        for level in range(LEVELS + 1):
            size = 2 ** (level + 1) if level < LEVELS else NROW
            mine = (lax.rem(r, size) == 2**level) if level < LEVELS else (r == 0)

            @pl.when(mine)
            def _():
                base = (r // size) * size

                def spread(j, carry):
                    t_copy(level, j, base + lax.rem(r - base + j, size)).start()
                    return carry

                lax.fori_loop(1, size, spread, 0)

    tops()
    compute()
    swap()
    share()
    spread_tops()

    for d in (1, 3, 2):
        y_copy(d).wait_recv()
    for i in range(RB):
        total = image[i]
        for d in range(1, NY):
            total = total + yrecv[d, i].astype(jnp.float32)
        image[i] = total

    lane0 = lax.broadcasted_iota(jnp.int32, (RHS, TILE), 1) == 0
    plain = jnp.concatenate([jnp.where(lane0, 0.0, image[i]) for i in range(RB)], axis=0)
    result = split_dot(plain * fac_ref[...], s_ref[...])

    top = jnp.zeros((RHS, 128), jnp.float32)
    for level in range(LEVELS + 1):
        @pl.when(targets[level] != r)
        def _():
            pltpu.make_async_copy(tsend, trecv.at[level], t_rs.at[level]).wait()

        @pl.when(targets[level] == r)
        def _():
            trecv[level] = tsend[...]

    for level in range(LEVELS + 1):
        size = 2 ** (level + 1) if level < LEVELS else NROW
        weight = size**-0.5
        if level < LEVELS:
            weight = jnp.where(lax.rem(r, size) < size // 2, weight, -weight)
        top = top + trecv[level] * weight

    back = [top] + [image[i, :, :128] for i in range(1, RB)]
    stride = RB // 2
    while stride >= 1:
        for p in range(0, RB, 2 * stride):
            u, v = back[p], back[p + stride]
            back[p], back[p + stride] = (u + v) * ROOT_HALF, (u - v) * ROOT_HALF
        stride //= 2
    for b in range(RB):
        level0 = jnp.broadcast_to(back[b][:, :1] * (TILE**-0.5), (RHS, TILE))
        out_ref[:, b * TILE : (b + 1) * TILE] = result[b * RHS : (b + 1) * RHS] + level0

    for level in range(LEVELS + 1):
        @pl.when(targets[level] != r)
        def _():
            f_copy(level, targets[level]).wait_send()
    for h in range(NPART):
        stage_a_done(h)
    for m, h in order:
        sends_done(m, h)
    for d in range(NY):
        k_copy(d).wait_send()
    for d in range(1, NCOL):
        u_copy(d).wait_send()
    for d in range(1, NY):
        y_copy(d).wait_send()
    for level in range(LEVELS + 1):
        size = 2 ** (level + 1) if level < LEVELS else NROW
        mine = (lax.rem(r, size) == 2**level) if level < LEVELS else (r == 0)

        @pl.when(mine)
        def _():
            def sent(j, carry):
                pltpu.make_async_copy(tsend, tsend, t_ss.at[j]).wait()
                return carry

            lax.fori_loop(1, size, sent, 0)


def local(sources, tiles, tile_row, tile_col, tile_count):
    table, factor = sign_table(TILE)
    s_mat = jnp.asarray(table, jnp.bfloat16)
    st_mat = jnp.asarray(table.T.copy(), jnp.bfloat16)
    fac = jnp.asarray(factor[None, :], jnp.float32)
    vmem = pl.BlockSpec(memory_space=pltpu.VMEM)
    hbm = pl.BlockSpec(memory_space=pltpu.HBM)
    f32, b16 = jnp.float32, jnp.bfloat16
    dma = pltpu.SemaphoreType.DMA
    return pl.pallas_call(
        kernel,
        out_shape=jax.ShapeDtypeStruct((RHS, RB * TILE), f32),
        in_specs=[hbm] * 8,
        out_specs=vmem,
        scratch_shapes=[
            pltpu.SMEM((1, 1, SLOTS), jnp.int32),
            pltpu.SMEM((1, 1, SLOTS), jnp.int32),
            pltpu.SMEM((1, 1), jnp.int32),
            pltpu.VMEM((1, 1, SLOTS), jnp.int32),
            pltpu.VMEM((1, 1, SLOTS), jnp.int32),
            pltpu.VMEM((TILE, TILE), b16),
            pltpu.VMEM((TILE, TILE), b16),
            pltpu.VMEM((1, TILE), f32),
            pltpu.VMEM((RHS, RB * TILE), f32),
            pltpu.VMEM((SLOTS, TILE, TILE), b16),
            pltpu.VMEM((RB, RHS, TILE), b16),
            pltpu.VMEM((NCOL, NX * RB, RHS, TILE), b16),
            pltpu.VMEM((SLOTS + 1, NCOL, RHS, TILE), f32),
            pltpu.VMEM((NY, RB, RHS, TILE), f32),
            pltpu.VMEM((NY, RB, RHS, TILE), f32),
            pltpu.VMEM((NY, RB, RHS, TILE), b16),
            pltpu.VMEM((NY, RB, RHS, TILE), b16),
            pltpu.VMEM((RB, RHS, TILE), f32),
            pltpu.VMEM((RHS, 128), f32),
            pltpu.VMEM((NROW, RHS, 128), f32),
            pltpu.VMEM((RHS, 128), f32),
            pltpu.VMEM((RHS, 128), f32),
            pltpu.VMEM((LEVELS + 1, RHS, 128), f32),
            pltpu.VMEM((NX * RB, TILE), f32),
            pltpu.VMEM((NCOL, RHS, 128), f32),
            pltpu.VMEM((NCOL, RHS, 128), f32),
            pltpu.SMEM((SLOTS,), jnp.int32),
            pltpu.SMEM((RB,), jnp.int32),
            dma((10,)),
            dma((LEVELS + 1,)),
            dma((NROW,)),
            dma((NPART * NZ,)),
            dma((NPART * NCOL,)),
            dma((NPART,)),
            dma((NPART * 2 * NCOL,)),
            dma((NPART * 2 * NCOL,)),
            dma((NPART * NCOL,)),
            dma((NPART * NCOL,)),
            dma((NY,)),
            dma((NY,)),
            dma((NY,)),
            dma((NY,)),
            dma((NROW,)),
            dma((LEVELS + 1,)),
            dma((NCOL,)),
            dma((NCOL,)),
        ],
        compiler_params=pltpu.CompilerParams(
            collective_id=0, has_side_effects=True, vmem_limit_bytes=64 * 2**20
        ),
    )(sources, tiles, tile_row, tile_col, tile_count, st_mat, s_mat, fac)


def solution(mesh):
    return jax.shard_map(
        local,
        mesh=mesh,
        in_specs=(
            P("col", "row"),
            P("row", "col", None, None, None),
            P("row", "col", None),
            P("row", "col", None),
            P("row", "col"),
        ),
        out_specs=P("col", "row"),
        check_vma=False,
    )
```

time: 61.7 us -> 56.4 us (0.914)
  Pallas kernels: 59.4 us -> 54 us
    pallas_call x1, Pallas kernels: 59.4 us -> 54 us  [local(): pl.pallas_call(kernel, out_shape=jax.ShapeDtypeStruct((RHS, RB * TILE), f...]
where the time goes in v3:
time: 56.4 us; the launch traced here: 56.3 us
  Pallas kernels  54 us (96%)
  local copies, waits for them, and re-layouts  1.57 us (3%)
  between operations  0.66 us (1%)
    pallas_call x1, Pallas kernels, local(): pl.pallas_call(kernel, out_shape=jax.ShapeDtypeStruct((RHS, RB * TILE), f...  54 us
    unnamed x1, local copies, waits for them, and re-layouts  1.57 us

profile of v3, /device:TPU:1, one launch (start us, length us, event | category | flops | bytes accessed | tf_op | source)
XLA Modules:
  0.0 56.3 jit_solution(4911298033837138995)
XLA Ops:
  0.7 54.0 %shard_map.82 = f32[16,2048]{1,0:T(8,128)} custom-call(f32[16,2048]{1,0:T(8,128)} %src_hbm.1, bf16[1,1,48,256,256]{4,3,2,1,0:T(8,128)(2,1)} %tiles_hbm.1, s32[1,1,48]{2,1,0:T(1,128)} %trow_hbm.1, s32[1,1,48]{2,1,0:T(1,128)} %tcol_hbm.1, s32[1,1]{1,0:T(1,128)S(6)} %copy.10.tcnt_hbm, bf16[256,256]{1,0:T(8,128)(2,1)} %constant.7.clone.st_hbm, ...), custom_call_target="tpu_custom_call" | custom-call | tf_op jit(solution)/shard_map/pallas_call | solution.py:485
  54.7 1.6 %copy.11 = f32[16,2048]{1,0:T(8,128)} copy(f32[16,2048]{1,0:T(8,128)} %shard_map.82) | data formatting | bytes 262144

commit v4 on v3

--- a/solution.py
+++ b/solution.py
@@ -21,6 +21,7 @@
 LAG = 8
 BEFORE = 2
 MIDDLE = 6
+LATER = 13
 
 
 def direct(m, h):
@@ -59,8 +60,8 @@
     out_ref,
     trow, tcol, tcnt, trow_v, tcol_v, st_ref, s_ref, fac_ref,
     src, tiles, wav, xa, run, part, recvk, ysend, yrecv, image,
-    fsend, frecv, facc, tsend, trecv, column, upart, urecv, prev, last,
-    ld_sem, f_ss, f_rs, a_ss, a_rs, l_sem, b_ss, b_rs, r_ss, r_rs, k_ss, k_rs, y_ss, y_rs, t_ss, t_rs, u_ss, u_rs,
+    fsend, frecv, facc, column, erecv, combo, full, upart, prev, last,
+    ld_sem, f_ss, f_rs, a_ss, a_rs, l_sem, b_ss, b_rs, r_ss, r_rs, k_ss, k_rs, y_ss, y_rs, e_ss, e_rs,
 ):
     r = lax.axis_index("row")
     c = lax.axis_index("col")
@@ -83,8 +84,9 @@
         return carry
 
     lax.fori_loop(0, NCOL, signal_source, 0)
-    for d in range(1, NCOL):
-        pl.semaphore_signal(bar, inc=1, device_id=(r, lax.rem(c + d, NCOL)), device_id_type=MESH)
+    pl.semaphore_signal(bar, inc=1, device_id=(r, y * NK + 1 - k), device_id_type=MESH)
+    for d in range(1, NY):
+        pl.semaphore_signal(bar, inc=1, device_id=(r, lax.rem(y + d, NY) * NK + k), device_id_type=MESH)
 
     pairs = (
         (trow_hbm, trow), (tcol_hbm, tcol), (tcnt_hbm, tcnt), (src_hbm, src), (st_hbm, st_ref), (fac_hbm, fac_ref),
@@ -133,7 +135,7 @@
         wav[b, :, 128:] = blocks[b][:, 128:].astype(jnp.bfloat16)
     fsend[...] = coarse[0]
 
-    pl.semaphore_wait(bar, NROW - 1 + NCOL - 1 + NCOL - jnp.where(z == c, 1, 0))
+    pl.semaphore_wait(bar, NROW - 1 + NY + NCOL - jnp.where(z == c, 1, 0))
 
     def f_copy(level, target):
         return pltpu.make_async_remote_copy(
@@ -309,9 +311,85 @@
         preferred_element_type=jnp.float32,
     )
 
-    serve_range(MIDDLE, len(order) + LAG)
+    def e_copy(ref, slot, j, target):
+        return pltpu.make_async_remote_copy(
+            src_ref=ref, dst_ref=erecv.at[slot], send_sem=e_ss.at[j], recv_sem=e_rs.at[slot],
+            device_id=(target, c), device_id_type=MESH,
+        )
+
+    def owners(act):
+        for level in range(LEVELS + 1):
+            size = 2 ** (level + 1) if level < LEVELS else NROW
+            jump = 1 if level < 2 else NX
+            mine = (lax.rem(r, size) == 2**level) if level < LEVELS else (r == 0)
+
+            @pl.when(mine)
+            def _():
+                def each(j, carry):
+                    base = (r // size) * size
+                    act(e_copy(column, level, j, base + lax.rem(r - base + j * jump, size)))
+                    return carry
+
+                lax.fori_loop(1, size // jump, each, 0)
+
+    def heirs(act):
+        for j in range(1, NX):
+            act(e_copy(combo, LEVELS + 1, NZ + j, r + j))
+
+    def arrive(levels):
+        for level in levels:
+            @pl.when(targets[level] != r)
+            def _():
+                wait_for(erecv.at[level], e_rs.at[level])
+
+            @pl.when(targets[level] == r)
+            def _():
+                erecv[level] = column[...]
+
+    def weighted(levels):
+        total = jnp.zeros((NX * RB, TILE), jnp.float32)
+        for level in levels:
+            size = 2 ** (level + 1) if level < LEVELS else NROW
+            weight = size**-0.5
+            if level < LEVELS:
+                weight = jnp.where(lax.rem(r, size) < size // 2, weight, -weight)
+            total = total + erecv[level] * weight
+        return total
+
+    owners(lambda copy: copy.start())
+    serve_range(MIDDLE, LATER)
+
+    @pl.when(x == 0)
+    def _():
+        arrive(range(2, LEVELS + 1))
+        combo[...] = weighted(range(2, LEVELS + 1))
+        heirs(lambda copy: copy.start())
+
+    serve_range(LATER, len(order) + LAG)
+
+    @pl.when(x != 0)
+    def _():
+        wait_for(erecv.at[LEVELS + 1], e_rs.at[LEVELS + 1])
+        full[...] = erecv[LEVELS + 1]
+
+    @pl.when(x == 0)
+    def _():
+        full[...] = combo[...]
+
+    arrive(range(2))
+    full[...] = full[...] + weighted(range(2))
+
     for m, h in order:
         finish(m, h)
+
+    def top():
+        def add(b, total):
+            side = xa[:, pl.ds(b, 1)].reshape(NCOL * RHS, TILE).astype(jnp.float32)
+            return total + side * full[pl.ds(b, 1), :]
+
+        total = lax.fori_loop(0, NX * RB, add, jnp.zeros((NCOL * RHS, TILE), jnp.float32), unroll=4)
+        value = jnp.sum(total, axis=1, keepdims=True)
+        upart[...] = jnp.broadcast_to(value, (NCOL * RHS, 128)).reshape(NCOL, RHS, 128)
 
     def compute():
         def step(t, carry):
@@ -337,15 +415,21 @@
 
     def swap():
         for d in (2, 1, 3, 0):
+            to = lax.rem(y + d, NY) * NK + 1 - k
             for i in range(RB):
-                part[d, i] = run[last[i], lax.rem(y + d, NY) * NK + 1 - k]
+                part[d, i] = run[last[i], to]
+            part[d, 0, :, :128] = jnp.where(first, upart[to], part[d, 0, :, :128])
             k_copy(d).start()
 
     def share():
         for d in (2, 1, 3, 0):
             k_copy(d).wait_recv()
+            to = lax.rem(y + d, NY) * NK + k
             for i in range(RB):
-                total = run[last[i], lax.rem(y + d, NY) * NK + k] + recvk[d, i]
+                total = run[last[i], to]
+                if i == 0:
+                    total = jnp.where(lane0, jnp.concatenate([upart[to]] * 2, axis=1), total)
+                total = total + recvk[d, i]
                 if d:
                     ysend[d, i] = total.astype(jnp.bfloat16)
                 else:
@@ -353,59 +437,11 @@
             if d:
                 y_copy(d).start()
 
-    def u_copy(d):
-        to = lax.rem(c + d, NCOL)
-        return pltpu.make_async_remote_copy(
-            src_ref=upart.at[to], dst_ref=urecv.at[c], send_sem=u_ss.at[d], recv_sem=u_rs.at[c],
-            device_id=(r, to), device_id_type=MESH,
-        )
-
-    def tops():
-        def add(b, total):
-            side = xa[:, pl.ds(b, 1)].reshape(NCOL * RHS, TILE).astype(jnp.float32)
-            return total + side * column[pl.ds(b, 1), :]
-
-        total = lax.fori_loop(0, NX * RB, add, jnp.zeros((NCOL * RHS, TILE), jnp.float32), unroll=4)
-        value = jnp.sum(total, axis=1, keepdims=True)
-        upart[...] = jnp.broadcast_to(value, (NCOL * RHS, 128)).reshape(NCOL, RHS, 128)
-        for d in (4, 5, 3, 6, 2, 7, 1):
-            u_copy(d).start()
-
-    def t_copy(slot, j, target):
-        return pltpu.make_async_remote_copy(
-            src_ref=tsend, dst_ref=trecv.at[slot], send_sem=t_ss.at[j], recv_sem=t_rs.at[slot],
-            device_id=(target, c), device_id_type=MESH,
-        )
-
-    def spread_tops():
-        urecv[c] = upart[c]
-        for d in range(1, NCOL):
-            sender = lax.rem(c + d, NCOL)
-            wait_for(urecv.at[sender], u_rs.at[sender])
-        total = urecv[0]
-        for sender in range(1, NCOL):
-            total = total + urecv[sender]
-        tsend[...] = total
-        for level in range(LEVELS + 1):
-            size = 2 ** (level + 1) if level < LEVELS else NROW
-            mine = (lax.rem(r, size) == 2**level) if level < LEVELS else (r == 0)
-
-            @pl.when(mine)
-            def _():
-                base = (r // size) * size
-
-                def spread(j, carry):
-                    t_copy(level, j, base + lax.rem(r - base + j, size)).start()
-                    return carry
-
-                lax.fori_loop(1, size, spread, 0)
-
-    tops()
+    lane0 = lax.broadcasted_iota(jnp.int32, (RHS, TILE), 1) == 0
+    top()
     compute()
     swap()
     share()
-    spread_tops()
-
     for d in (1, 3, 2):
         y_copy(d).wait_recv()
     for i in range(RB):
@@ -414,37 +450,19 @@
             total = total + yrecv[d, i].astype(jnp.float32)
         image[i] = total
 
-    lane0 = lax.broadcasted_iota(jnp.int32, (RHS, TILE), 1) == 0
-    plain = jnp.concatenate([jnp.where(lane0, 0.0, image[i]) for i in range(RB)], axis=0)
-    result = split_dot(plain * fac_ref[...], s_ref[...])
-
-    top = jnp.zeros((RHS, 128), jnp.float32)
-    for level in range(LEVELS + 1):
-        @pl.when(targets[level] != r)
-        def _():
-            pltpu.make_async_copy(tsend, trecv.at[level], t_rs.at[level]).wait()
-
-        @pl.when(targets[level] == r)
-        def _():
-            trecv[level] = tsend[...]
-
-    for level in range(LEVELS + 1):
-        size = 2 ** (level + 1) if level < LEVELS else NROW
-        weight = size**-0.5
-        if level < LEVELS:
-            weight = jnp.where(lax.rem(r, size) < size // 2, weight, -weight)
-        top = top + trecv[level] * weight
-
-    back = [top] + [image[i, :, :128] for i in range(1, RB)]
+    back = [image[i, :, :128] for i in range(RB)]
     stride = RB // 2
     while stride >= 1:
         for p in range(0, RB, 2 * stride):
             u, v = back[p], back[p + stride]
             back[p], back[p + stride] = (u + v) * ROOT_HALF, (u - v) * ROOT_HALF
         stride //= 2
+    for i in range(RB):
+        image[i, :, :128] = jnp.where(first, back[i], image[i, :, :128])
+    coefs = jnp.concatenate([image[i] for i in range(RB)], axis=0)
+    result = split_dot(coefs * fac_ref[...], s_ref[...])
     for b in range(RB):
-        level0 = jnp.broadcast_to(back[b][:, :1] * (TILE**-0.5), (RHS, TILE))
-        out_ref[:, b * TILE : (b + 1) * TILE] = result[b * RHS : (b + 1) * RHS] + level0
+        out_ref[:, b * TILE : (b + 1) * TILE] = result[b * RHS : (b + 1) * RHS]
 
     for level in range(LEVELS + 1):
         @pl.when(targets[level] != r)
@@ -456,21 +474,13 @@
         sends_done(m, h)
     for d in range(NY):
         k_copy(d).wait_send()
-    for d in range(1, NCOL):
-        u_copy(d).wait_send()
     for d in range(1, NY):
         y_copy(d).wait_send()
-    for level in range(LEVELS + 1):
-        size = 2 ** (level + 1) if level < LEVELS else NROW
-        mine = (lax.rem(r, size) == 2**level) if level < LEVELS else (r == 0)
-
-        @pl.when(mine)
-        def _():
-            def sent(j, carry):
-                pltpu.make_async_copy(tsend, tsend, t_ss.at[j]).wait()
-                return carry
-
-            lax.fori_loop(1, size, sent, 0)
+    owners(lambda copy: copy.wait_send())
+
+    @pl.when(x == 0)
+    def _():
+        heirs(lambda copy: copy.wait_send())
 
 
 def local(sources, tiles, tile_row, tile_col, tile_count):
@@ -509,10 +519,10 @@
             pltpu.VMEM((RHS, 128), f32),
             pltpu.VMEM((NROW, RHS, 128), f32),
             pltpu.VMEM((RHS, 128), f32),
-            pltpu.VMEM((RHS, 128), f32),
-            pltpu.VMEM((LEVELS + 1, RHS, 128), f32),
             pltpu.VMEM((NX * RB, TILE), f32),
-            pltpu.VMEM((NCOL, RHS, 128), f32),
+            pltpu.VMEM((LEVELS + 2, NX * RB, TILE), f32),
+            pltpu.VMEM((NX * RB, TILE), f32),
+            pltpu.VMEM((NX * RB, TILE), f32),
             pltpu.VMEM((NCOL, RHS, 128), f32),
             pltpu.SMEM((SLOTS,), jnp.int32),
             pltpu.SMEM((RB,), jnp.int32),
@@ -530,10 +540,8 @@
             dma((NY,)),
             dma((NY,)),
             dma((NY,)),
-            dma((NROW,)),
-            dma((LEVELS + 1,)),
-            dma((NCOL,)),
-            dma((NCOL,)),
+            dma((NZ + NX,)),
+            dma((LEVELS + 2,)),
         ],
         compiler_params=pltpu.CompilerParams(
             collective_id=0, has_side_effects=True, vmem_limit_bytes=64 * 2**20

time: 56.4 us -> 53.5 us (0.949)
  Pallas kernels: 54 us -> 51.1 us
    pallas_call x1, Pallas kernels: 54 us -> 51.1 us  [local(): pl.pallas_call(kernel, out_shape=jax.ShapeDtypeStruct((RHS, RB * TILE), f...]
where the time goes in v4:
time: 53.5 us; the launch traced here: 53.4 us
  Pallas kernels  51.1 us (96%)
  local copies, waits for them, and re-layouts  1.57 us (3%)
  between operations  0.66 us (1%)
    pallas_call x1, Pallas kernels, local(): pl.pallas_call(kernel, out_shape=jax.ShapeDtypeStruct((RHS, RB * TILE), f...  51.1 us
    unnamed x1, local copies, waits for them, and re-layouts  1.57 us

profile of v4, /device:TPU:1, one launch (start us, length us, event | category | flops | bytes accessed | tf_op | source)
XLA Modules:
  0.0 53.4 jit_solution(1996413094507779263)
XLA Ops:
  0.7 51.1 %shard_map.82 = f32[16,2048]{1,0:T(8,128)} custom-call(f32[16,2048]{1,0:T(8,128)} %src_hbm.1, bf16[1,1,48,256,256]{4,3,2,1,0:T(8,128)(2,1)} %tiles_hbm.1, s32[1,1,48]{2,1,0:T(1,128)} %trow_hbm.1, s32[1,1,48]{2,1,0:T(1,128)} %tcol_hbm.1, s32[1,1]{1,0:T(1,128)S(6)} %copy.10.tcnt_hbm, bf16[256,256]{1,0:T(8,128)(2,1)} %constant.7.clone.st_hbm, ...), custom_call_target="tpu_custom_call" | custom-call | tf_op jit(solution)/shard_map/pallas_call | solution.py:495
  51.8 1.6 %copy.11 = f32[16,2048]{1,0:T(8,128)} copy(f32[16,2048]{1,0:T(8,128)} %shard_map.82) | data formatting | bytes 262144

commit v5 on v4

--- a/solution.py
+++ b/solution.py
@@ -20,6 +20,7 @@
 NPART = len(PARTS)
 LAG = 8
 BEFORE = 2
+CUTS = 4
 MIDDLE = 6
 LATER = 13
 
@@ -33,15 +34,12 @@
 
 def sign_table(extent):
     signs = np.zeros((extent, extent), np.float32)
-    factor = np.zeros((extent,), np.float64)
     signs[0] = 1.0
-    factor[0] = extent**-0.5
     for n in range(1, extent):
         low = n & -n
         signs[n, n - low : n] = 1.0
         signs[n, n : n + low] = -1.0
-        factor[n] = (2.0 * low) ** -0.5
-    return signs, factor.astype(np.float32)
+    return signs
 
 
 def split_dot(values, matrix):
@@ -56,11 +54,11 @@
 
 
 def kernel(
-    src_hbm, tiles_hbm, trow_hbm, tcol_hbm, tcnt_hbm, st_hbm, s_hbm, fac_hbm,
+    src_hbm, tiles_hbm, trow_hbm, tcol_hbm, tcnt_hbm, st_hbm, s_hbm,
     out_ref,
-    trow, tcol, tcnt, trow_v, tcol_v, st_ref, s_ref, fac_ref,
+    trow, tcol, tcnt, trow_v, tcol_v, st_ref, s_ref,
     src, tiles, wav, xa, run, part, recvk, ysend, yrecv, image,
-    fsend, frecv, facc, column, erecv, combo, full, upart, prev, last,
+    fsend, frecv, facc, column, erecv, combo, full, picked, upart, prev, last,
     ld_sem, f_ss, f_rs, a_ss, a_rs, l_sem, b_ss, b_rs, r_ss, r_rs, k_ss, k_rs, y_ss, y_rs, e_ss, e_rs,
 ):
     r = lax.axis_index("row")
@@ -89,7 +87,7 @@
         pl.semaphore_signal(bar, inc=1, device_id=(r, lax.rem(y + d, NY) * NK + k), device_id_type=MESH)
 
     pairs = (
-        (trow_hbm, trow), (tcol_hbm, tcol), (tcnt_hbm, tcnt), (src_hbm, src), (st_hbm, st_ref), (fac_hbm, fac_ref),
+        (trow_hbm, trow), (tcol_hbm, tcol), (tcnt_hbm, tcnt), (src_hbm, src), (st_hbm, st_ref),
         (s_hbm, s_ref), (tiles_hbm.at[0, 0], tiles), (trow_hbm, trow_v), (tcol_hbm, tcol_v),
     )
     loads = [pltpu.make_async_copy(a, b, ld_sem.at[i]) for i, (a, b) in enumerate(pairs)]
@@ -116,10 +114,16 @@
         last[i] = lasts[i]
     run[0] = jnp.zeros((NCOL, RHS, TILE), jnp.float32)
 
-    for load in loads[3:6]:
+    place = lax.broadcasted_iota(jnp.int32, (1, TILE), 1)
+    factor = jnp.full((1, TILE), TILE**-0.5, jnp.float32)
+    low = 1
+    while low < TILE:
+        factor = jnp.where(lax.rem(place, 2 * low) == low, (2.0 * low) ** -0.5, factor)
+        low *= 2
+    for load in loads[3:5]:
         load.wait()
     stacked = jnp.concatenate([src[:, b * TILE : (b + 1) * TILE] for b in range(RB)], axis=0)
-    coef = split_dot(stacked, st_ref[...]) * fac_ref[...]
+    coef = split_dot(stacked, st_ref[...]) * factor
     blocks = [coef[b * RHS : (b + 1) * RHS] for b in range(RB)]
     coarse = [blocks[b][:, :128] for b in range(RB)]
     stride = 1
@@ -292,9 +296,9 @@
 
     wav[0, :, :128] = jnp.where(first, facc[...], wav[0, :, :128].astype(jnp.float32)).astype(jnp.bfloat16)
     stage_a(NPART - 1)
-    serve_range(BEFORE, MIDDLE)
-
-    for load in loads[6:]:
+    serve_range(BEFORE, MIDDLE - CUTS + 1)
+
+    for load in loads[5:]:
         load.wait()
     slot_lane = lax.broadcasted_iota(jnp.int32, (TILE, 128), 1)
 
@@ -302,7 +306,13 @@
         value = tiles[t, :, :128].astype(jnp.float32)
         return jnp.where(slot_lane == t, jnp.broadcast_to(value[:, :1], (TILE, 128)), found)
 
-    found = lax.fori_loop(0, SLOTS, pick, jnp.zeros((TILE, 128), jnp.float32))
+    found = jnp.zeros((TILE, 128), jnp.float32)
+    for cut in range(CUTS):
+        found = lax.fori_loop(cut * SLOTS // CUTS, (cut + 1) * SLOTS // CUTS, pick, found)
+        picked[...] = found
+        if cut < CUTS - 1:
+            serve_range(MIDDLE - CUTS + 1 + cut, MIDDLE - CUTS + 2 + cut)
+        found = picked[...]
     slot = lax.broadcasted_iota(jnp.int32, (NX * RB, SLOTS), 1)
     block = lax.broadcasted_iota(jnp.int32, (NX * RB, SLOTS), 0)
     hit = (tcol_v[0] == block) & (trow_v[0] == 0) & (slot < count)
@@ -460,7 +470,7 @@
     for i in range(RB):
         image[i, :, :128] = jnp.where(first, back[i], image[i, :, :128])
     coefs = jnp.concatenate([image[i] for i in range(RB)], axis=0)
-    result = split_dot(coefs * fac_ref[...], s_ref[...])
+    result = split_dot(coefs * factor, s_ref[...])
     for b in range(RB):
         out_ref[:, b * TILE : (b + 1) * TILE] = result[b * RHS : (b + 1) * RHS]
 
@@ -484,10 +494,9 @@
 
 
 def local(sources, tiles, tile_row, tile_col, tile_count):
-    table, factor = sign_table(TILE)
+    table = sign_table(TILE)
     s_mat = jnp.asarray(table, jnp.bfloat16)
     st_mat = jnp.asarray(table.T.copy(), jnp.bfloat16)
-    fac = jnp.asarray(factor[None, :], jnp.float32)
     vmem = pl.BlockSpec(memory_space=pltpu.VMEM)
     hbm = pl.BlockSpec(memory_space=pltpu.HBM)
     f32, b16 = jnp.float32, jnp.bfloat16
@@ -495,7 +504,7 @@
     return pl.pallas_call(
         kernel,
         out_shape=jax.ShapeDtypeStruct((RHS, RB * TILE), f32),
-        in_specs=[hbm] * 8,
+        in_specs=[hbm] * 7,
         out_specs=vmem,
         scratch_shapes=[
             pltpu.SMEM((1, 1, SLOTS), jnp.int32),
@@ -505,7 +514,6 @@
             pltpu.VMEM((1, 1, SLOTS), jnp.int32),
             pltpu.VMEM((TILE, TILE), b16),
             pltpu.VMEM((TILE, TILE), b16),
-            pltpu.VMEM((1, TILE), f32),
             pltpu.VMEM((RHS, RB * TILE), f32),
             pltpu.VMEM((SLOTS, TILE, TILE), b16),
             pltpu.VMEM((RB, RHS, TILE), b16),
@@ -523,10 +531,11 @@
             pltpu.VMEM((LEVELS + 2, NX * RB, TILE), f32),
             pltpu.VMEM((NX * RB, TILE), f32),
             pltpu.VMEM((NX * RB, TILE), f32),
+            pltpu.VMEM((TILE, 128), f32),
             pltpu.VMEM((NCOL, RHS, 128), f32),
             pltpu.SMEM((SLOTS,), jnp.int32),
             pltpu.SMEM((RB,), jnp.int32),
-            dma((10,)),
+            dma((9,)),
             dma((LEVELS + 1,)),
             dma((NROW,)),
             dma((NPART * NZ,)),
@@ -544,9 +553,9 @@
             dma((LEVELS + 2,)),
         ],
         compiler_params=pltpu.CompilerParams(
-            collective_id=0, has_side_effects=True, vmem_limit_bytes=64 * 2**20
+            collective_id=0, has_side_effects=True, vmem_limit_bytes=55000 * 2**10
         ),
-    )(sources, tiles, tile_row, tile_col, tile_count, st_mat, s_mat, fac)
+    )(sources, tiles, tile_row, tile_col, tile_count, st_mat, s_mat)
 
 
 def solution(mesh):

time: 53.5 us -> 52.7 us (0.985)
  Pallas kernels: 51.1 us -> 49.9 us
    pallas_call x1, Pallas kernels: 51.1 us -> 49.9 us  [local(): pl.pallas_call(kernel, out_shape=jax.ShapeDtypeStruct((RHS, RB * TILE), f...]
    unnamed x1 -> x5, local copies, waits for them, and re-layouts: 1.57 us -> 1.96 us
where the time goes in v5:
time: 52.7 us; the launch traced here: 52.6 us
  Pallas kernels  49.9 us (95%)
  local copies, waits for them, and re-layouts  1.96 us (4%)
  between operations  0.67 us (1%)
    pallas_call x1, Pallas kernels, local(): pl.pallas_call(kernel, out_shape=jax.ShapeDtypeStruct((RHS, RB * TILE), f...  49.9 us
    unnamed x5, local copies, waits for them, and re-layouts  1.96 us

profile of v5, /device:TPU:1, one launch (start us, length us, event | category | flops | bytes accessed | tf_op | source)
XLA Modules:
  0.0 52.6 jit_solution(17532647996526757999)
XLA Ops:
  0.7 0.0 copy-start
  0.7 0.6 %copy-done = s32[1,1,48]{2,1,0:T(1,128)S(1)} copy-done((s32[1,1,48]{2,1,0:T(1,128)S(1)}, s32[1,1,48]{2,1,0:T(1,128)}, u32[]{:S(2)}) %copy-start) | copy-done | bytes 216
  1.3 0.0 copy-start.1
  1.3 0.7 %copy-done.1 = s32[1,1,48]{2,1,0:T(1,128)S(1)} copy-done((s32[1,1,48]{2,1,0:T(1,128)S(1)}, s32[1,1,48]{2,1,0:T(1,128)}, u32[]{:S(2)}) %copy-start.1) | copy-done | bytes 216
  2.0 49.9 %shard_map.73 = f32[16,2048]{1,0:T(8,128)S(1)} custom-call(f32[16,2048]{1,0:T(8,128)} %src_hbm.1, bf16[1,1,48,256,256]{4,3,2,1,0:T(8,128)(2,1)} %tiles_hbm.1, s32[1,1,48]{2,1,0:T(1,128)S(1)} %copy-done, s32[1,1,48]{2,1,0:T(1,128)S(1)} %copy-done.1, s32[1,1]{1,0:T(1,128)S(6)} %copy.9.tcnt_hbm, bf16[256,256]{1,0:T(8,128)(2,1)} %constant.5.clone.st_hbm, ...), custom_call_target="tpu_custom_call" | custom-call | tf_op jit(solution)/shard_map/pallas_call | solution.py:504
  51.9 0.7 %copy.10 = f32[16,2048]{1,0:T(8,128)} copy(f32[16,2048]{1,0:T(8,128)S(1)} %shard_map.73) | data formatting | bytes 262144
Async XLA Ops:
  0.7 0.7 %copy-start = (s32[1,1,48]{2,1,0:T(1,128)S(1)}, s32[1,1,48]{2,1,0:T(1,128)}, u32[]{:S(2)}) copy-start(s32[1,1,48]{2,1,0:T(1,128)} %trow_hbm.1) | copy-start | bytes 580
  1.3 0.7 %copy-start.1 = (s32[1,1,48]{2,1,0:T(1,128)S(1)}, s32[1,1,48]{2,1,0:T(1,128)}, u32[]{:S(2)}) copy-start(s32[1,1,48]{2,1,0:T(1,128)} %tcol_hbm.1) | copy-start | bytes 580

commit v6 on v5

--- a/solution.py
+++ b/solution.py
@@ -19,7 +19,7 @@
 PARTS = ((4, 4), (0, 4))
 NPART = len(PARTS)
 LAG = 8
-BEFORE = 2
+BEFORE = 1
 CUTS = 4
 MIDDLE = 6
 LATER = 13

time: 52.7 us -> 52.7 us (level)
  no operation moved by 1% of the time
where the time goes in v6:
time: 52.7 us; the launch traced here: 52.6 us
  Pallas kernels  50 us (95%)
  local copies, waits for them, and re-layouts  1.96 us (4%)
  between operations  0.67 us (1%)
    pallas_call x1, Pallas kernels, local(): pl.pallas_call(kernel, out_shape=jax.ShapeDtypeStruct((RHS, RB * TILE), f...  50 us
    unnamed x5, local copies, waits for them, and re-layouts  1.96 us

profile of v6, /device:TPU:1, one launch (start us, length us, event | category | flops | bytes accessed | tf_op | source)
XLA Modules:
  0.0 52.6 jit_solution(5590988465903126988)
XLA Ops:
  0.7 0.0 copy-start
  0.7 0.6 %copy-done = s32[1,1,48]{2,1,0:T(1,128)S(1)} copy-done((s32[1,1,48]{2,1,0:T(1,128)S(1)}, s32[1,1,48]{2,1,0:T(1,128)}, u32[]{:S(2)}) %copy-start) | copy-done | bytes 216
  1.3 0.0 copy-start.1
  1.3 0.7 %copy-done.1 = s32[1,1,48]{2,1,0:T(1,128)S(1)} copy-done((s32[1,1,48]{2,1,0:T(1,128)S(1)}, s32[1,1,48]{2,1,0:T(1,128)}, u32[]{:S(2)}) %copy-start.1) | copy-done | bytes 216
  2.0 50.0 %shard_map.73 = f32[16,2048]{1,0:T(8,128)S(1)} custom-call(f32[16,2048]{1,0:T(8,128)} %src_hbm.1, bf16[1,1,48,256,256]{4,3,2,1,0:T(8,128)(2,1)} %tiles_hbm.1, s32[1,1,48]{2,1,0:T(1,128)S(1)} %copy-done, s32[1,1,48]{2,1,0:T(1,128)S(1)} %copy-done.1, s32[1,1]{1,0:T(1,128)S(6)} %copy.9.tcnt_hbm, bf16[256,256]{1,0:T(8,128)(2,1)} %constant.5.clone.st_hbm, ...), custom_call_target="tpu_custom_call" | custom-call | tf_op jit(solution)/shard_map/pallas_call | solution.py:504
  52.0 0.7 %copy.10 = f32[16,2048]{1,0:T(8,128)} copy(f32[16,2048]{1,0:T(8,128)S(1)} %shard_map.73) | data formatting | bytes 262144
Async XLA Ops:
  0.7 0.7 %copy-start = (s32[1,1,48]{2,1,0:T(1,128)S(1)}, s32[1,1,48]{2,1,0:T(1,128)}, u32[]{:S(2)}) copy-start(s32[1,1,48]{2,1,0:T(1,128)} %trow_hbm.1) | copy-start | bytes 580
  1.3 0.7 %copy-start.1 = (s32[1,1,48]{2,1,0:T(1,128)S(1)}, s32[1,1,48]{2,1,0:T(1,128)}, u32[]{:S(2)}) copy-start(s32[1,1,48]{2,1,0:T(1,128)} %tcol_hbm.1) | copy-start | bytes 580
